TPU v7x, 256 devices: a whole 4x4x8 slice. The times are simulated.
256 devices in a mesh: run: 4 (over y), space: 64 (over z, x, core).
Axes of the slice: x: 4, y: 4, z: 8, core: 2. Of those that a mesh axis runs over, the one named last changes fastest.
Arguments:
- snapshots: bfloat16 [131072, 1024], P('space', 'run'), may hold values from -6 to 6
- run_counts: int32 [4], P('run'), may hold values from 128 to 256
- route_counts: int32 [64, 64], replicated, may hold values from 16 to 48, as said below
Outputs:
- modes: bfloat16 [131072, 256], P('space', 'run')
Inputs may be any that keep to these rules, and one draw needn't show every extreme that they name: route_counts[s, d] depends only on (d - s) mod 64; each of its rows and columns sums to 2048.
All inputs are finite; a program needn't handle non-finite values.
Results may differ from a plain program's by a relative error of at most 0.0069.
The roundings to bfloat16 on the way count: a program that leaves them out, or rounds other values in their place, can miss the bound.
Values may be sent and summed in bfloat16 or wider, within the bound.
No kernel may reach another device: no remote copies, remote signals or barrier semaphores. Data moves between devices by JAX's collectives and lax.ppermute only.
A program may use at most 64 MiB of HBM per device.

v0:
```python
import functools
import math

import jax
import jax.numpy as jnp
from jax import lax
from jax.experimental import pallas as pl
from jax.experimental.pallas import tpu as pltpu
from jax.sharding import PartitionSpec as P

ITERS = 2
NS_STEPS = 8
BF = jnp.bfloat16
F32 = jnp.float32


def dot(a, b):
    return lax.dot_general(a, b, (((1,), (0,)), ((), ())), preferred_element_type=F32)


def dot_t(a, b):
    return lax.dot_general(a, b, (((0,), (0,)), ((), ())), preferred_element_type=F32)


def dot_nt(a, b):
    return lax.dot_general(a, b, (((1,), (1,)), ((), ())), preferred_element_type=F32)


def split(x):
    hi = x.astype(BF)
    return hi, (x - hi.astype(F32)).astype(BF)


def mul(a, b, op=dot):
    return op(a[0], b[0]) + (op(a[0], b[1]) + op(a[1], b[0]))


def half_mul(a, b, op=dot):
    return op(a[0], b) + op(a[1], b)


def half_mul_t(b, a):
    return dot_t(b, a[0]) + dot_t(b, a[1])


def solve(grams, eye):
    root = 1.0 / math.sqrt(2.0)
    gs = [(split(a), split(b), split(c)) for a, b, c in grams]
    heads = [((a + b) * root, (b.T + c) * root) for a, b, c in grams]
    for sweep in range(ITERS):
        scaled = []
        for pt, pb in heads:
            norm = lax.rsqrt(jnp.sum(pt * pt + pb * pb, keepdims=True) + 1e-06)
            scaled.append((split(pt * norm), split(pb * norm)))
        moments = [mul(st, st, dot_t) + mul(sb, sb, dot_t) for st, sb in scaled]
        turns = None
        ahead, fill = [], []
        for (a, b, c), (st, sb) in zip(gs, scaled):
            cell = [None] * 4
            ahead.append(cell)
            for n, f in enumerate((lambda a=a, st=st: mul(a, st), lambda b=b, sb=sb: mul(b, sb),
                                   lambda b=b, st=st: mul(b, st, dot_t), lambda c=c, sb=sb: mul(c, sb))):
                fill.append((cell, n, f))
        if sweep + 1 == ITERS:
            fill = []
        for k in range(NS_STEPS):
            last = k == NS_STEPS - 1
            halves = [split(m) for m in moments]
            weights = [1.5 * eye - 0.5 * m for m in moments]
            if not last:
                squares = [mul(h, h) for h in halves]
            turns = weights if k == 0 else [mul(split(t), split(w)) for t, w in zip(turns, weights)]
            for cell, n, f in fill[:len(grams)]:
                cell[n] = f()
            fill = fill[len(grams):]
            if not last:
                moments = [mul(h, split(2.25 * eye - 1.5 * m + 0.25 * q)) for h, m, q in zip(halves, moments, squares)]
        turns = [split(t) for t in turns]
        if sweep + 1 < ITERS:
            scaled = [(split(c[0] + c[1]), split(c[2] + c[3])) for c in ahead]
        heads = [(mul(st, t), mul(sb, t)) for (st, sb), t in zip(scaled, turns)]
    return heads


def identity(width):
    rows = lax.broadcasted_iota(jnp.int32, (width, width), 0)
    return (rows == lax.broadcasted_iota(jnp.int32, (width, width), 1)).astype(F32)


def level0_kernel(place_ref, *refs):
    parts, (near_ref, far_ref, outer_ref, own_ref, rest_ref, sems) = refs[:4], refs[4:]
    core = place_ref[1]
    copies = []
    for j, ref in enumerate((own_ref, rest_ref)):
        for k, slot in enumerate((core, 1 - core)):
            copies.append(pltpu.make_async_copy(parts[2 * j + k], ref.at[slot], sems.at[2 * j + k]))
    for c in copies:
        c.start()
    for c in copies:
        c.wait()
    width = near_ref.shape[1]
    half = width // 2

    def block(ref, n):
        at = slice(n * half, (n + 1) * half)
        return jnp.concatenate([ref[0, :, at], ref[1, :, at]], axis=1)

    near = (block(own_ref, 0), block(own_ref, 1), block(rest_ref, 0))
    far = (block(rest_ref, 2), block(rest_ref, 3), block(rest_ref, 1))
    grams = [near, far]
    bases = [(t.astype(BF), b.astype(BF)) for t, b in solve(grams, identity(width))]
    for i, ref in enumerate((near_ref, far_ref)):
        t, b = bases[i]
        ref[:width] = t
        ref[width:] = b
        g = [split(x) for x in grams[i]]
        up = half_mul(g[0], t) + half_mul(g[1], b)
        down = half_mul(g[1], t, dot_t) + half_mul(g[2], b)
        outer_ref[i] = half_mul_t(t, split(up)) + half_mul_t(b, split(down))


def level0(place, parts, width):
    half = width // 2
    return pl.pallas_call(
        level0_kernel,
        out_shape=[
            jax.ShapeDtypeStruct((2 * width, width), BF),
            jax.ShapeDtypeStruct((2 * width, width), BF),
            jax.ShapeDtypeStruct((2, width, width), F32),
        ],
        in_specs=[pl.BlockSpec(memory_space=pltpu.SMEM)] + [pl.BlockSpec(memory_space=pl.ANY)] * 4,
        scratch_shapes=[
            pltpu.VMEM((2, width, 3 * half), F32),
            pltpu.VMEM((2, width, 4 * half), F32),
            pltpu.SemaphoreType.DMA((4,)),
        ],
        compiler_params=pltpu.CompilerParams(vmem_limit_bytes=40 * 2**20),
        cost_estimate=pl.CostEstimate(flops=12 * 10**9, bytes_accessed=2 * 2**20, transcendentals=0),
        name="level0",
    )(place, *parts)


def level1_kernel(place_ref, near_ref, far_ref, outer_ref, c0_ref, c1_ref, c2_ref, c3_ref, last_ref, between_ref):
    run = place_ref[0]
    width = near_ref.shape[1]
    near = (near_ref[:width], near_ref[width:])
    far = (far_ref[width:], far_ref[:width])

    def between(first, second, f0, f1, s0, s1):
        (ft, fb), (st, sb) = first, second
        to_s1, to_s0, from_s0, from_s1 = (split(x[...]) for x in (f0, f1, s0, s1))
        up = half_mul(to_s1, sb) + half_mul(from_s1, st, dot_t)
        down = half_mul(to_s0, st) + half_mul(from_s0, sb, dot_t)
        return half_mul_t(ft, split(up)) + half_mul_t(fb, split(down))

    @pl.when(run < 2)
    def _():
        between_ref[...] = between(near, far, c0_ref, c1_ref, c2_ref, c3_ref)

    @pl.when(run >= 2)
    def _():
        between_ref[...] = between(far, near, c2_ref, c3_ref, c0_ref, c1_ref).T

    [(t, b)] = solve([(outer_ref[0], between_ref[...], outer_ref[1])], identity(width))
    quarter = last_ref.shape[0]
    pick_row = lax.broadcasted_iota(jnp.int32, (quarter, width), 0)
    pick_col = lax.broadcasted_iota(jnp.int32, (quarter, width), 1)
    pick = (pick_col == pick_row + run * quarter).astype(F32).astype(BF)
    last_ref[:, :width] = dot_nt(pick, t.astype(BF)).astype(BF)
    last_ref[:, width:] = dot_nt(pick, b.astype(BF)).astype(BF)


def level1(place, near, far, outer, crosses, width, quarter):
    return pl.pallas_call(
        level1_kernel,
        out_shape=jax.ShapeDtypeStruct((quarter, 2 * width), BF),
        in_specs=[pl.BlockSpec(memory_space=pltpu.SMEM)] + [pl.BlockSpec(memory_space=pltpu.VMEM)] * 7,
        out_specs=pl.BlockSpec(memory_space=pltpu.VMEM),
        scratch_shapes=[pltpu.VMEM((width, width), F32)],
        compiler_params=pltpu.CompilerParams(vmem_limit_bytes=40 * 2**20),
        cost_estimate=pl.CostEstimate(flops=8 * 10**9, bytes_accessed=2 * 2**20, transcendentals=0),
        name="level1",
    )(place, near, far, outer, *crosses)


def pack_kernel(shards, slots, counts_ref, rows_ref, out_ref, wide_ref):
    cells = rows_ref.shape[0]
    strips, _, lanes = wide_ref.shape
    pad = wide_ref.shape[1] - cells
    for h in range(strips):
        at = slice(h * lanes, (h + 1) * lanes)
        wide_ref[h, pl.ds(0, cells)] = rows_ref[:, at].astype(F32)
        wide_ref[h, pl.ds(cells, pad)] = jnp.zeros((pad, lanes), F32)

    def one(d, start):
        at = pl.ds(pl.multiple_of(d * slots, 16), slots)
        for h in range(strips):
            out_ref[at, h * lanes:(h + 1) * lanes] = wide_ref[h, pl.ds(start, slots)].astype(BF)
        return jnp.minimum(start + counts_ref[d], cells)

    lax.fori_loop(0, shards, one, jnp.int32(0), unroll=4)


def unpack_kernel(shards, slots, counts_ref, in_ref, out_ref, turned_ref, wide_ref):
    cells = out_ref.shape[0]
    half = cells // 2
    strips, _, lanes = wide_ref.shape

    def one(s, start):
        at = pl.ds(pl.multiple_of(s * slots, 16), slots)
        for h in range(strips):
            wide_ref[h, pl.ds(start, slots)] = in_ref[at, h * lanes:(h + 1) * lanes].astype(F32)
        return jnp.minimum(start + counts_ref[s], cells)

    lax.fori_loop(0, shards, one, jnp.int32(0), unroll=4)
    for h in range(strips):
        at = slice(h * lanes, (h + 1) * lanes)
        for k in range(2):
            rows = wide_ref[h, pl.ds(k * half, half)].astype(BF)
            out_ref[pl.ds(k * half, half), at] = rows
            turned_ref[pl.ds((1 - k) * half, half), at] = rows


def rotate_kernel(tiles, own, p1, p2a, p2b, p3, near_ref, far_ref, last_ref, out_ref):
    width = near_ref.shape[1]

    def turn(p2):
        near = (dot(own[...], near_ref[:width]) + dot(p1[...], near_ref[width:])).astype(BF)
        far = (dot(p3[...], far_ref[:width]) + dot(p2[...], far_ref[width:])).astype(BF)
        out_ref[...] = (dot_nt(last_ref[:, :width], near) + dot_nt(last_ref[:, width:], far)).astype(BF)

    @pl.when(pl.program_id(0) < tiles)
    def _():
        turn(p2a)

    @pl.when(pl.program_id(0) >= tiles)
    def _():
        turn(p2b)


def rotate(own, p1, p2a, p2b, p3, near, far, last):
    quarter = last.shape[0]
    tiles = 2
    cells, width = own.shape
    tile = cells // (2 * tiles)
    straight = pl.BlockSpec((tile, width), lambda i: (i, 0))
    low = pl.BlockSpec((tile, width), lambda i: (jnp.minimum(i, tiles - 1), 0))
    high = pl.BlockSpec((tile, width), lambda i: (jnp.maximum(i - tiles, 0), 0))
    swapped = pl.BlockSpec((tile, width), lambda i: (jnp.where(i < tiles, i + tiles, i - tiles), 0))
    whole = [pl.BlockSpec(x.shape, lambda i: (0, 0)) for x in (near, far, last)]
    return pl.pallas_call(
        functools.partial(rotate_kernel, tiles),
        grid=(2 * tiles,),
        out_shape=jax.ShapeDtypeStruct((quarter, cells), BF),
        in_specs=[straight, straight, low, high, swapped] + whole,
        out_specs=pl.BlockSpec((quarter, tile), lambda i: (0, i)),
        compiler_params=pltpu.CompilerParams(vmem_limit_bytes=40 * 2**20),
        name="rotate",
    )(own, p1, p2a, p2b, p3, near, far, last)


def local_call(kernel, shapes, specs, scratch, name):
    outs = [jax.ShapeDtypeStruct(shape, BF) for shape in shapes]
    return pl.pallas_call(
        kernel,
        out_shape=outs,
        in_specs=[pl.BlockSpec(memory_space=m) for m in specs],
        out_specs=[pl.BlockSpec(memory_space=pltpu.VMEM) for _ in outs],
        scratch_shapes=scratch,
        compiler_params=pltpu.CompilerParams(vmem_limit_bytes=40 * 2**20),
        name=name,
    )


def body(snapshots, run_counts, route_counts):
    cells, width = snapshots.shape
    shards = lax.axis_size("space")
    runs = lax.axis_size("run")
    slots = 3 * cells // (2 * shards)
    run = lax.axis_index("run")
    spot = lax.axis_index("space")
    core = lax.rem(spot, 2)
    groups = [[2 * i + c for i in range(shards // 2)] for c in range(2)]

    def across(x, mask):
        return lax.ppermute(x, "run", [(r, r ^ mask) for r in range(runs)])

    def other_core(x):
        return lax.ppermute(x, "space", [(s, s ^ 1) for s in range(shards)])

    send = lax.dynamic_index_in_dim(route_counts, spot, 0, keepdims=False)
    recv = lax.dynamic_index_in_dim(route_counts, spot, 1, keepdims=False)
    smem, vmem = pltpu.SMEM, pltpu.VMEM
    wide = [pltpu.VMEM((width // 128, cells + 64, 128), F32)]
    keep = jnp.arange(width, dtype=jnp.int32) < run_counts[0]
    own = jnp.where(keep[None, :], snapshots, jnp.zeros((), BF))
    p1, p3 = across(own, 1), across(own, 3)
    [packed] = local_call(
        functools.partial(pack_kernel, shards, slots), [(shards * slots, width)], [smem, vmem], wide, "pack"
    )(send, own)
    arrived = lax.all_to_all(packed.reshape(shards, slots, width), "space", 0, 0, tiled=True)

    left = jnp.where(run < 2, own, p1)
    blocks = [dot_t(own, own), dot_t(own, p1), dot_t(left, p3)]
    half = width // 2

    def side(first):
        return jnp.concatenate([jnp.where(first, b[:, :half], b[:, half:]) for b in blocks], axis=1)

    mine = side(core == 0) + other_core(side(core == 1))
    mine, arrived = lax.optimization_barrier((mine, arrived))
    cut = mine.shape[1]
    routed, turned = local_call(
        functools.partial(unpack_kernel, shards, slots), [(cells, width)] * 2, [smem, vmem], wide, "unpack"
    )(recv, arrived.reshape(shards * slots, width))
    pieces = mine.reshape(shards // 2, -1, cut)
    pieces = lax.all_to_all(pieces, "space", 0, 0, tiled=True, axis_index_groups=groups)
    r1, r3 = across(routed, 1), across(turned, 3)
    pieces, routed = lax.optimization_barrier((pieces, routed))
    total = jnp.sum(pieces, axis=0)
    pieces = lax.all_to_all(
        jnp.broadcast_to(total, pieces.shape), "space", 0, 0, tiled=True, axis_index_groups=groups
    )
    spread = pieces.reshape(width, cut)
    r2a, r2b = across(r1[:cells // 2], 3), across(r3[:cells // 2], 1)
    spread, r1, r3 = lax.optimization_barrier((spread, r1, r3))
    swap = other_core(spread)
    g3 = across(spread[:, :width], 3)
    g1 = across(spread[:, :half], 1)
    g2 = across(spread[:, :half], 2)
    c0 = jnp.where(
        core == 0,
        jnp.concatenate([spread[:, width:], swap[:, width:]], axis=1),
        jnp.concatenate([swap[:, width:], spread[:, width:]], axis=1),
    )
    g1, g2, g3, c0, swap, r2a, r2b = lax.optimization_barrier((g1, g2, g3, c0, swap, r2a, r2b))
    mine = jnp.concatenate([g1, g2, g3], axis=1)
    crosses = [c0, across(c0, 1), across(c0, 2), across(c0, 3)]
    place = jnp.stack([run, core]).astype(jnp.int32)
    near, far, outer = level0(place, [spread, swap, mine, other_core(mine)], width)
    last = level1(place, near, far, outer, crosses, width, width // runs)
    return rotate(routed, r1, r2a, r2b, r3, near, far, last).T


def solution(mesh):
    in_specs = (P("space", "run"), P("run"), P())
    out_specs = P("space", "run")
    return jax.shard_map(body, mesh=mesh, in_specs=in_specs, out_specs=out_specs, check_vma=False)
```

profile of v0, /device:TPU:1, one launch (start us, length us, event | category | flops | bytes accessed | tf_op | source)
XLA Modules:
  0.0 153.2 jit_solution(13879921464419965420)
XLA Ops:
  0.7 1.3 broadcast_select_fusion.rows_ref
  2.0 2.2 %pack.1 = bf16[3072,256]{1,0:T(8,128)(2,1)} custom-call(s32[64]{0:T(128)S(1)} %dynamic-slice_bitcast_fusion.counts_ref, bf16[2048,256]{1,0:T(8,128)(2,1)S(1)} %broadcast_select_fusion.rows_ref), custom_call_target="tpu_custom_call" | custom-call | tf_op jit(solution)/shard_map/pack/pallas_call | solution.py:298
  4.2 13.0 %all-to-all-start = ((bf16[64,48,256]{2,1,0:T(8,128)(2,1)}), bf16[64,48,256]{2,1,0:T(8,128)(2,1)S(1)}, u32[]{:S(2)}, u32[]{:S(2)}) async-start(bf16[64,48,256]{2,1,0:T(8,128)(2,1)} %bitcast.2), calls=%async_computation | async-start | bytes 3145728 | tf_op jit(solution)/shard_map/all_to_all | solution.py:301
  17.2 2.8 %collective-permute-start.1 = (bf16[2048,256]{1,0:T(8,128)(2,1)S(1)}, bf16[2048,256]{1,0:T(8,128)(2,1)}, u32[]{:S(2)}, u32[]{:S(2)}) collective-permute-start(bf16[2048,256]{1,0:T(8,128)(2,1)S(1)} %broadcast_select_fusion.rows_ref), channel_id=1, source_target_pairs={{0,192},{64,128},{128,64},{192,0},{1,193},{65,129},{129,65},{193,1... | collective-permute-start | bytes 3145736 | tf_op jit(solution)/shard_map/ppermute | solution.py:286
  20.0 0.0 collective-permute-start
  20.0 0.5 fusion.4
  20.6 22.4 %collective-permute-done.1 = bf16[2048,256]{1,0:T(8,128)(2,1)} collective-permute-done((bf16[2048,256]{1,0:T(8,128)(2,1)S(1)}, bf16[2048,256]{1,0:T(8,128)(2,1)}, u32[]{:S(2)}, u32[]{:S(2)}) %collective-permute-start.1) | collective-permute-done | bytes 1048608 | tf_op jit(solution)/shard_map/ppermute | solution.py:286
  43.0 1.1 collective-permute-done
  44.1 1.8 %fusion = f32[256,256]{0,1:T(8,128)S(1)} fusion(bf16[2048,256]{1,0:T(8,128)(2,1)} %collective-permute-done.1, bf16[2048,256]{1,0:T(8,128)(2,1)S(1)} %broadcast_select_fusion.rows_ref, bf16[2048,256]{1,0:T(8,128)(2,1)} %collective-permute-done, pred[]{:T(512)S(6)} %lt.19), kind=kOutput, calls=%fused_computation | convolution fusion | flops 268959744 | bytes 3407873 | tf_op jit(solution)/shard_map/dot_general | solution.py:22
  45.9 1.7 %fusion.5 = f32[256,256]{0,1:T(8,128)S(1)} fusion(bf16[2048,256]{1,0:T(8,128)(2,1)S(1)} %broadcast_select_fusion.rows_ref, bf16[2048,256]{1,0:T(8,128)(2,1)} %collective-permute-done), kind=kOutput, calls=%fused_computation.22 | convolution fusion | flops 268435456 | bytes 2359296 | tf_op jit(solution)/shard_map/dot_general | solution.py:22
  47.7 1.7 %collective-permute-start.2 = (f32[256,384]{0,1:T(8,128)S(1)}, f32[256,384]{0,1:T(8,128)S(1)}, u32[]{:S(2)}, u32[]{:S(2)}) collective-permute-start(f32[256,384]{0,1:T(8,128)S(1)} %pad_maximum_fusion), channel_id=1, source_target_pairs={{0,1},{1,0},{2,3},{3,2},{4,5},{5,4},{6,7},{7,6},{8,9},{9,8},{10,11... | collective-permute-start | bytes 1179656 | tf_op jit(solution)/shard_map/ppermute | solution.py:289
  49.4 1.3 collective-permute-done.2
  50.7 0.1 maximum_add_fusion
  50.8 5.4 %all-to-all-done = bf16[64,48,256]{2,1,0:T(8,128)(2,1)S(1)} async-done(((bf16[64,48,256]{2,1,0:T(8,128)(2,1)}), bf16[64,48,256]{2,1,0:T(8,128)(2,1)S(1)}, u32[]{:S(2)}, u32[]{:S(2)}) %all-to-all-start) | async-done | bytes 1572896 | tf_op jit(solution)/shard_map/all_to_all | solution.py:301
  56.2 0.9 copy.4
  57.1 5.2 %all-to-all-start.1 = ((f32[32,8,384]{2,1,0:T(8,128)}), f32[32,8,384]{2,1,0:T(8,128)S(1)}, u32[]{:S(2)}, u32[]{:S(2)}) async-start(f32[32,8,384]{2,1,0:T(8,128)} %bitcast.3), calls=%async_computation.1 | async-start | bytes 786432 | tf_op jit(solution)/shard_map/all_to_all | solution.py:317
  62.3 0.2 dynamic-slice_reduce_fusion.counts_ref
  62.5 2.4 %unpack.1 = (bf16[2048,256]{1,0:T(8,128)(2,1)}, bf16[2048,256]{1,0:T(8,128)(2,1)}) custom-call(s32[64]{0:T(128)S(1)} %dynamic-slice_reduce_fusion.counts_ref, bf16[3072,256]{1,0:T(8,128)(2,1)S(1)} %bitcast.16), custom_call_target="tpu_custom_call" | custom-call | tf_op jit(solution)/shard_map/unpack/pallas_call | solution.py:313
  64.9 1.3 collective-permute-start.3
  66.2 1.9 %collective-permute-start.4 = (bf16[2048,256]{1,0:T(8,128)(2,1)}, bf16[2048,256]{1,0:T(8,128)(2,1)S(1)}, u32[]{:S(2)}, u32[]{:S(2)}) collective-permute-start(bf16[2048,256]{1,0:T(8,128)(2,1)} %get-tuple-element.29), channel_id=1, source_target_pairs={{0,192},{64,128},{128,64},{192,0},{1,193},{65,129},{129,65},{193,1... | collective-permute-start | bytes 3145736 | tf_op jit(solution)/shard_map/ppermute | solution.py:286
  68.1 8.1 %all-to-all-done.1 = f32[32,8,384]{2,1,0:T(8,128)S(1)} async-done(((f32[32,8,384]{2,1,0:T(8,128)}), f32[32,8,384]{2,1,0:T(8,128)S(1)}, u32[]{:S(2)}, u32[]{:S(2)}) %all-to-all-start.1) | async-done | bytes 393248 | tf_op jit(solution)/shard_map/all_to_all | solution.py:317
  76.3 0.8 broadcast_in_dim.18
  77.1 4.9 %all-to-all-start.2 = ((f32[32,8,384]{2,1,0:T(8,128)}), f32[32,8,384]{2,1,0:T(8,128)S(1)}, u32[]{:S(2)}, u32[]{:S(2)}) async-start(f32[32,8,384]{2,1,0:T(8,128)} %broadcast_in_dim.18), calls=%async_computation.2 | async-start | bytes 786432 | tf_op jit(solution)/shard_map/all_to_all | solution.py:321
  82.0 6.8 %collective-permute-done.3.p1 = bf16[2048,256]{1,0:T(8,128)(2,1)S(1)} collective-permute-done((bf16[2048,256]{1,0:T(8,128)(2,1)}, bf16[2048,256]{1,0:T(8,128)(2,1)S(1)}, u32[]{:S(2)}, u32[]{:S(2)}) %collective-permute-start.3) | collective-permute-done | bytes 1048608 | tf_op jit(solution)/shard_map/ppermute | solution.py:286
  88.7 0.8 slice.64
  89.5 2.7 %collective-permute-start.9 = (bf16[1024,256]{1,0:T(8,128)(2,1)}, bf16[1024,256]{1,0:T(8,128)(2,1)S(1)}, u32[]{:S(2)}, u32[]{:S(2)}) collective-permute-start(bf16[1024,256]{1,0:T(8,128)(2,1)} %slice.64), channel_id=1, source_target_pairs={{0,192},{64,128},{128,64},{192,0},{1,193},{65,129},{129,65},{193,1... | collective-permute-start | bytes 1572872 | tf_op jit(solution)/shard_map/ppermute | solution.py:286
  92.3 0.0 collective-permute-done.4.p3
  92.3 0.8 slice.65
  93.1 1.7 %all-to-all-done.2 = f32[32,8,384]{2,1,0:T(8,128)S(1)} async-done(((f32[32,8,384]{2,1,0:T(8,128)}), f32[32,8,384]{2,1,0:T(8,128)S(1)}, u32[]{:S(2)}, u32[]{:S(2)}) %all-to-all-start.2) | async-done | bytes 393248 | tf_op jit(solution)/shard_map/all_to_all | solution.py:321
  94.9 3.3 %collective-permute-start.8 = (f32[256,384]{1,0:T(8,128)S(1)}, f32[256,384]{1,0:T(8,128)S(1)}, u32[]{:S(2)}, u32[]{:S(2)}) collective-permute-start(f32[256,384]{1,0:T(8,128)S(1)} %bitcast.17), channel_id=1, source_target_pairs={{0,1},{1,0},{2,3},{3,2},{4,5},{5,4},{6,7},{7,6},{8,9},{9,8},{10,11... | collective-permute-start | bytes 1179656 | tf_op jit(solution)/shard_map/ppermute | solution.py:289
  98.2 2.8 %collective-permute-start.7 = (f32[256,256]{1,0:T(8,128)S(1)}, f32[256,256]{1,0:T(8,128)S(1)}, u32[]{:S(2)}, u32[]{:S(2)}) collective-permute-start(f32[256,256]{1,0:T(8,128)S(1)} %slice.52), channel_id=1, source_target_pairs={{0,192},{64,128},{128,64},{192,0},{1,193},{65,129},{129,65},{193,1... | collective-permute-start | bytes 786440 | tf_op jit(solution)/shard_map/ppermute | solution.py:286
  101.1 0.1 collective-permute-start.5
  101.2 1.3 collective-permute-start.6
  102.5 0.0 collective-permute-done.9.p2a
  102.5 2.1 %collective-permute-done.10.p2b = bf16[1024,256]{1,0:T(8,128)(2,1)} collective-permute-done((bf16[1024,256]{1,0:T(8,128)(2,1)}, bf16[1024,256]{1,0:T(8,128)(2,1)}, u32[]{:S(2)}, u32[]{:S(2)}) %collective-permute-start.10) | collective-permute-done | bytes 524320 | tf_op jit(solution)/shard_map/ppermute | solution.py:286
  104.6 2.8 %collective-permute-done.5 = f32[256,128]{1,0:T(8,128)S(1)} collective-permute-done((f32[256,128]{1,0:T(8,128)S(1)}, f32[256,128]{1,0:T(8,128)S(1)}, u32[]{:S(2)}, u32[]{:S(2)}) %collective-permute-start.5) | collective-permute-done | bytes 131104 | tf_op jit(solution)/shard_map/ppermute | solution.py:286
  107.4 2.7 %collective-permute-done.6 = f32[256,128]{1,0:T(8,128)S(1)} collective-permute-done((f32[256,128]{1,0:T(8,128)S(1)}, f32[256,128]{1,0:T(8,128)S(1)}, u32[]{:S(2)}, u32[]{:S(2)}) %collective-permute-start.6) | collective-permute-done | bytes 131104 | tf_op jit(solution)/shard_map/ppermute | solution.py:286
  110.1 0.0 collective-permute-done.7
  110.2 3.8 %collective-permute-start.11 = (f32[256,512]{1,0:T(8,128)S(1)}, f32[256,512]{1,0:T(8,128)S(1)}, u32[]{:S(2)}, u32[]{:S(2)}) collective-permute-start(f32[256,512]{1,0:T(8,128)S(1)} %constant_dynamic-update-slice_fusion.refs_2_), channel_id=1, source_target_pairs={{0,1},{1,0},{2,3},{3,2},{4,5},{5,4},{6,7},{7,6},{8,9},{9,8},{10,11... | collective-permute-start | bytes 1572872 | tf_op jit(solution)/shard_map/ppermute | solution.py:289
  113.9 0.1 pad_add_fusion.place_ref
  114.0 0.0 collective-permute-start.12
  114.1 3.8 %collective-permute-start.13 = (f32[256,256]{1,0:T(8,128)S(1)}, f32[256,256]{1,0:T(8,128)S(1)}, u32[]{:S(2)}, u32[]{:S(2)}) collective-permute-start(f32[256,256]{1,0:T(8,128)S(1)} %maximum_select_fusion.c0_ref), channel_id=1, source_target_pairs={{0,128},{64,192},{128,0},{192,64},{1,129},{65,193},{129,1},{193,65... | collective-permute-start | bytes 786440 | tf_op jit(solution)/shard_map/ppermute | solution.py:286
  117.9 0.0 collective-permute-done.11.refs_3_
  117.9 16.8 %level0.1 = (bf16[512,256]{1,0:T(8,128)(2,1)S(1)}, bf16[512,256]{1,0:T(8,128)(2,1)S(1)}, f32[2,256,256]{2,1,0:T(8,128)S(1)}) custom-call(s32[2]{0:T(128)S(1)} %pad_add_fusion.place_ref, f32[256,384]{1,0:T(8,128)S(1)} %bitcast.20, f32[256,384]{1,0:T(8,128)S(1)} %collective-permute-done.8.refs_1_, f32[256,512]{1,0:T(8,128)S(1)} %constant_dynamic-update-slice_fusion.refs_2_, ...), custom_call_target="tpu_custom_call" | custom-call | flops 12000000000 | bytes 2097152 | tf_op jit(solution)/shard_map/level0/pallas_call | solution.py:124
  134.7 0.0 collective-permute-done.12.c1_ref
  134.7 0.0 collective-permute-done.14.c3_ref
  134.7 13.7 %level1.1.last_ref = bf16[64,512]{1,0:T(8,128)(2,1)S(1)} custom-call(s32[2]{0:T(128)S(1)} %pad_add_fusion.place_ref, bf16[512,256]{1,0:T(8,128)(2,1)S(1)} %get-tuple-element.39.near_ref, bf16[512,256]{1,0:T(8,128)(2,1)S(1)} %get-tuple-element.40.far_ref, f32[2,256,256]{2,1,0:T(8,128)S(1)} %get-tuple-element.41.outer_ref, ...), custom_call_target="tpu_custom_call" | custom-call | flops 8000000000 | bytes 2097152 | tf_op jit(solution)/shard_map/level1/pallas_call | solution.py:174
  148.5 4.8 %rotate.1 = bf16[64,2048]{1,0:T(8,128)(2,1)} custom-call(bf16[2048,256]{1,0:T(8,128)(2,1)} %get-tuple-element.27.own, bf16[2048,256]{1,0:T(8,128)(2,1)S(1)} %collective-permute-done.3.p1, bf16[1024,256]{1,0:T(8,128)(2,1)S(1)} %collective-permute-done.9.p2a, bf16[1024,256]{1,0:T(8,128)(2,1)} %collective-permute-done.10.p2b, ...), custom_call_target="tpu_custom_call" | custom-call | tf_op jit(solution)/shard_map/rotate/pallas_call | solution.py:251
  (20 shorter events, 0.3 us)
Async XLA Ops:
  0.0 2.0 %copy-start = (s32[64,64]{1,0:T(8,128)S(1)}, s32[64,64]{1,0:T(8,128)}, u32[]{:S(2)}) copy-start(s32[64,64]{1,0:T(8,128)} %param.5) | copy-start | bytes 49156
  4.2 52.0 %all-to-all-start = ((bf16[64,48,256]{2,1,0:T(8,128)(2,1)}), bf16[64,48,256]{2,1,0:T(8,128)(2,1)S(1)}, u32[]{:S(2)}, u32[]{:S(2)}) async-start(bf16[64,48,256]{2,1,0:T(8,128)(2,1)} %bitcast.2), calls=%async_computation | async-start | bytes 3145728 | tf_op jit(solution)/shard_map/all_to_all | solution.py:301
  17.2 25.8 %collective-permute-start.1 = (bf16[2048,256]{1,0:T(8,128)(2,1)S(1)}, bf16[2048,256]{1,0:T(8,128)(2,1)}, u32[]{:S(2)}, u32[]{:S(2)}) collective-permute-start(bf16[2048,256]{1,0:T(8,128)(2,1)S(1)} %broadcast_select_fusion.rows_ref), channel_id=1, source_target_pairs={{0,192},{64,128},{128,64},{192,0},{1,193},{65,129},{129,65},{193,1... | collective-permute-start | bytes 3145736 | tf_op jit(solution)/shard_map/ppermute | solution.py:286
  20.0 24.1 %collective-permute-start = (bf16[2048,256]{1,0:T(8,128)(2,1)S(1)}, bf16[2048,256]{1,0:T(8,128)(2,1)}, u32[]{:S(2)}, u32[]{:S(2)}) collective-permute-start(bf16[2048,256]{1,0:T(8,128)(2,1)S(1)} %broadcast_select_fusion.rows_ref), channel_id=1, source_target_pairs={{0,64},{64,0},{128,192},{192,128},{1,65},{65,1},{129,193},{193,129... | collective-permute-start | bytes 3145736 | tf_op jit(solution)/shard_map/ppermute | solution.py:286
  47.7 3.1 %collective-permute-start.2 = (f32[256,384]{0,1:T(8,128)S(1)}, f32[256,384]{0,1:T(8,128)S(1)}, u32[]{:S(2)}, u32[]{:S(2)}) collective-permute-start(f32[256,384]{0,1:T(8,128)S(1)} %pad_maximum_fusion), channel_id=1, source_target_pairs={{0,1},{1,0},{2,3},{3,2},{4,5},{5,4},{6,7},{7,6},{8,9},{9,8},{10,11... | collective-permute-start | bytes 1179656 | tf_op jit(solution)/shard_map/ppermute | solution.py:289
  57.1 19.1 %all-to-all-start.1 = ((f32[32,8,384]{2,1,0:T(8,128)}), f32[32,8,384]{2,1,0:T(8,128)S(1)}, u32[]{:S(2)}, u32[]{:S(2)}) async-start(f32[32,8,384]{2,1,0:T(8,128)} %bitcast.3), calls=%async_computation.1 | async-start | bytes 786432 | tf_op jit(solution)/shard_map/all_to_all | solution.py:317
  64.9 23.8 %collective-permute-start.3 = (bf16[2048,256]{1,0:T(8,128)(2,1)}, bf16[2048,256]{1,0:T(8,128)(2,1)S(1)}, u32[]{:S(2)}, u32[]{:S(2)}) collective-permute-start(bf16[2048,256]{1,0:T(8,128)(2,1)} %get-tuple-element.27.own), channel_id=1, source_target_pairs={{0,64},{64,0},{128,192},{192,128},{1,65},{65,1},{129,193},{193,129... | collective-permute-start | bytes 3145736 | tf_op jit(solution)/shard_map/ppermute | solution.py:286
  66.2 26.1 %collective-permute-start.4 = (bf16[2048,256]{1,0:T(8,128)(2,1)}, bf16[2048,256]{1,0:T(8,128)(2,1)S(1)}, u32[]{:S(2)}, u32[]{:S(2)}) collective-permute-start(bf16[2048,256]{1,0:T(8,128)(2,1)} %get-tuple-element.29), channel_id=1, source_target_pairs={{0,192},{64,128},{128,64},{192,0},{1,193},{65,129},{129,65},{193,1... | collective-permute-start | bytes 3145736 | tf_op jit(solution)/shard_map/ppermute | solution.py:286
  77.1 17.8 %all-to-all-start.2 = ((f32[32,8,384]{2,1,0:T(8,128)}), f32[32,8,384]{2,1,0:T(8,128)S(1)}, u32[]{:S(2)}, u32[]{:S(2)}) async-start(f32[32,8,384]{2,1,0:T(8,128)} %broadcast_in_dim.18), calls=%async_computation.2 | async-start | bytes 786432 | tf_op jit(solution)/shard_map/all_to_all | solution.py:321
  89.5 13.0 %collective-permute-start.9 = (bf16[1024,256]{1,0:T(8,128)(2,1)}, bf16[1024,256]{1,0:T(8,128)(2,1)S(1)}, u32[]{:S(2)}, u32[]{:S(2)}) collective-permute-start(bf16[1024,256]{1,0:T(8,128)(2,1)} %slice.64), channel_id=1, source_target_pairs={{0,192},{64,128},{128,64},{192,0},{1,193},{65,129},{129,65},{193,1... | collective-permute-start | bytes 1572872 | tf_op jit(solution)/shard_map/ppermute | solution.py:286
  93.1 11.5 %collective-permute-start.10 = (bf16[1024,256]{1,0:T(8,128)(2,1)}, bf16[1024,256]{1,0:T(8,128)(2,1)}, u32[]{:S(2)}, u32[]{:S(2)}) collective-permute-start(bf16[1024,256]{1,0:T(8,128)(2,1)} %slice.65), channel_id=1, source_target_pairs={{0,64},{64,0},{128,192},{192,128},{1,65},{65,1},{129,193},{193,129... | collective-permute-start | bytes 1572872 | tf_op jit(solution)/shard_map/ppermute | solution.py:286
  94.9 6.3 %collective-permute-start.8 = (f32[256,384]{1,0:T(8,128)S(1)}, f32[256,384]{1,0:T(8,128)S(1)}, u32[]{:S(2)}, u32[]{:S(2)}) collective-permute-start(f32[256,384]{1,0:T(8,128)S(1)} %bitcast.17), channel_id=1, source_target_pairs={{0,1},{1,0},{2,3},{3,2},{4,5},{5,4},{6,7},{7,6},{8,9},{9,8},{10,11... | collective-permute-start | bytes 1179656 | tf_op jit(solution)/shard_map/ppermute | solution.py:289
  98.2 11.9 %collective-permute-start.7 = (f32[256,256]{1,0:T(8,128)S(1)}, f32[256,256]{1,0:T(8,128)S(1)}, u32[]{:S(2)}, u32[]{:S(2)}) collective-permute-start(f32[256,256]{1,0:T(8,128)S(1)} %slice.52), channel_id=1, source_target_pairs={{0,192},{64,128},{128,64},{192,0},{1,193},{65,129},{129,65},{193,1... | collective-permute-start | bytes 786440 | tf_op jit(solution)/shard_map/ppermute | solution.py:286
  101.1 6.3 %collective-permute-start.5 = (f32[256,128]{1,0:T(8,128)S(1)}, f32[256,128]{1,0:T(8,128)S(1)}, u32[]{:S(2)}, u32[]{:S(2)}) collective-permute-start(f32[256,128]{1,0:T(8,128)S(1)} %get-tuple-element.44), channel_id=1, source_target_pairs={{0,64},{64,0},{128,192},{192,128},{1,65},{65,1},{129,193},{193,129... | collective-permute-start | bytes 393224 | tf_op jit(solution)/shard_map/ppermute | solution.py:286
  101.2 8.9 %collective-permute-start.6 = (f32[256,128]{1,0:T(8,128)S(1)}, f32[256,128]{1,0:T(8,128)S(1)}, u32[]{:S(2)}, u32[]{:S(2)}) collective-permute-start(f32[256,128]{1,0:T(8,128)S(1)} %get-tuple-element.44), channel_id=1, source_target_pairs={{0,128},{64,192},{128,0},{192,64},{1,129},{65,193},{129,1},{193,65... | collective-permute-start | bytes 393224 | tf_op jit(solution)/shard_map/ppermute | solution.py:286
  110.2 7.7 %collective-permute-start.11 = (f32[256,512]{1,0:T(8,128)S(1)}, f32[256,512]{1,0:T(8,128)S(1)}, u32[]{:S(2)}, u32[]{:S(2)}) collective-permute-start(f32[256,512]{1,0:T(8,128)S(1)} %constant_dynamic-update-slice_fusion.refs_2_), channel_id=1, source_target_pairs={{0,1},{1,0},{2,3},{3,2},{4,5},{5,4},{6,7},{7,6},{8,9},{9,8},{10,11... | collective-permute-start | bytes 1572872 | tf_op jit(solution)/shard_map/ppermute | solution.py:289
  114.0 20.7 %collective-permute-start.12 = (f32[256,256]{1,0:T(8,128)S(1)}, f32[256,256]{1,0:T(8,128)S(1)}, u32[]{:S(2)}, u32[]{:S(2)}) collective-permute-start(f32[256,256]{1,0:T(8,128)S(1)} %maximum_select_fusion.c0_ref), channel_id=1, source_target_pairs={{0,64},{64,0},{128,192},{192,128},{1,65},{65,1},{129,193},{193,129... | collective-permute-start | bytes 786440 | tf_op jit(solution)/shard_map/ppermute | solution.py:286
  114.1 20.6 %collective-permute-start.13 = (f32[256,256]{1,0:T(8,128)S(1)}, f32[256,256]{1,0:T(8,128)S(1)}, u32[]{:S(2)}, u32[]{:S(2)}) collective-permute-start(f32[256,256]{1,0:T(8,128)S(1)} %maximum_select_fusion.c0_ref), channel_id=1, source_target_pairs={{0,128},{64,192},{128,0},{192,64},{1,129},{65,193},{129,1},{193,65... | collective-permute-start | bytes 786440 | tf_op jit(solution)/shard_map/ppermute | solution.py:286
  117.9 16.8 %collective-permute-start.14 = (f32[256,256]{1,0:T(8,128)S(1)}, f32[256,256]{1,0:T(8,128)S(1)}, u32[]{:S(2)}, u32[]{:S(2)}) collective-permute-start(f32[256,256]{1,0:T(8,128)S(1)} %maximum_select_fusion.c0_ref), channel_id=1, source_target_pairs={{0,192},{64,128},{128,64},{192,0},{1,193},{65,129},{129,65},{193,1... | collective-permute-start | bytes 786440 | tf_op jit(solution)/shard_map/ppermute | solution.py:286
where the time goes:
time: 154 us; the launch traced here: 153 us
  waiting for transfers between devices  54.4 us (35%)
  starting transfers between devices  48.8 us (32%)
  Pallas kernels  39.9 us (26%)
  matrix products  4.02 us (3%)
  local copies, waits for them, and re-layouts  3.66 us (2%)
  other arithmetic  1.59 us (1%)
    ppermute x12, waiting for transfers between devices, across(): return lax.ppermute(x, 'run', [(r, r ^ mask) for r in range(runs)])  37.9 us
    ppermute x12, starting transfers between devices, across(): return lax.ppermute(x, 'run', [(r, r ^ mask) for r in range(runs)])  16.8 us
    pallas_call x1, Pallas kernels, level0(): pl.pallas_call(level0_kernel, out_shape=[jax.ShapeDtypeStruct((2 * width,...  16.8 us
    pallas_call x1, Pallas kernels, level1(): pl.pallas_call(level1_kernel, out_shape=jax.ShapeDtypeStruct((quarter, 2...  13.7 us
    all_to_all x1, starting transfers between devices, body(): lax.all_to_all(packed.reshape(shards, slots, width), 'space', 0, 0, tiled...  13 us
    ppermute x3, starting transfers between devices, other_core(): return lax.ppermute(x, 'space', [(s, s ^ 1) for s in range(shards)])  8.82 us
    all_to_all x1, waiting for transfers between devices, body(): lax.all_to_all(pieces, 'space', 0, 0, tiled=True, axis_index_groups=groups)  8.1 us
    all_to_all x1, waiting for transfers between devices, body(): lax.all_to_all(packed.reshape(shards, slots, width), 'space', 0, 0, tiled...  5.39 us
  transfers between devices with their start and end apart: 18, of which 10 were waited for; matrix products, arithmetic and copies ran while one was open for 5% of the time, Pallas kernels for 13%

commit v1 on v0

--- a/solution.py
+++ b/solution.py
@@ -322,8 +322,8 @@
         jnp.broadcast_to(total, pieces.shape), "space", 0, 0, tiled=True, axis_index_groups=groups
     )
     spread = pieces.reshape(width, cut)
-    r2a, r2b = across(r1[:cells // 2], 3), across(r3[:cells // 2], 1)
-    spread, r1, r3 = lax.optimization_barrier((spread, r1, r3))
+    on1, on3 = r1[:cells // 2], r3[:cells // 2]
+    spread, r1, r3, on1, on3 = lax.optimization_barrier((spread, r1, r3, on1, on3))
     swap = other_core(spread)
     g3 = across(spread[:, :width], 3)
     g1 = across(spread[:, :half], 1)
@@ -333,11 +333,13 @@
         jnp.concatenate([spread[:, width:], swap[:, width:]], axis=1),
         jnp.concatenate([swap[:, width:], spread[:, width:]], axis=1),
     )
-    g1, g2, g3, c0, swap, r2a, r2b = lax.optimization_barrier((g1, g2, g3, c0, swap, r2a, r2b))
+    g1, g2, g3, c0, swap = lax.optimization_barrier((g1, g2, g3, c0, swap))
     mine = jnp.concatenate([g1, g2, g3], axis=1)
     crosses = [c0, across(c0, 1), across(c0, 2), across(c0, 3)]
     place = jnp.stack([run, core]).astype(jnp.int32)
     near, far, outer = level0(place, [spread, swap, mine, other_core(mine)], width)
+    near, on1, on3 = lax.optimization_barrier((near, on1, on3))
+    r2a, r2b = across(on1, 3), across(on3, 1)
     last = level1(place, near, far, outer, crosses, width, width // runs)
     return rotate(routed, r1, r2a, r2b, r3, near, far, last).T
 

time: 154 us -> 154 us (level)
  waiting for transfers between devices: 54.4 us -> 58.4 us
  starting transfers between devices: 48.8 us -> 45.7 us
    ppermute x3, starting transfers between devices: 8.82 us -> 5.83 us  [other_core(): return lax.ppermute(x, 'space', [(s, s ^ 1) for s in range(shards)])]
    ppermute x12, waiting for transfers between devices: 37.9 us -> 40.5 us  [across(): return lax.ppermute(x, 'run', [(r, r ^ mask) for r in range(runs)])]
  transfers between devices with their start and end apart: 18 -> 18, of which waited for: 10 -> 11; matrix products, arithmetic and copies ran while one was open for 5% -> 4% of each run, Pallas kernels for 13% -> 22%
where the time goes in v1:
time: 154 us; the launch traced here: 153 us
  waiting for transfers between devices  58.4 us (38%)
  starting transfers between devices  45.7 us (30%)
  Pallas kernels  39.9 us (26%)
  matrix products  4.02 us (3%)
  local copies, waits for them, and re-layouts  2.84 us (2%)
  other arithmetic  1.59 us (1%)
    ppermute x12, waiting for transfers between devices, across(): return lax.ppermute(x, 'run', [(r, r ^ mask) for r in range(runs)])  40.5 us
    pallas_call x1, Pallas kernels, level0(): pl.pallas_call(level0_kernel, out_shape=[jax.ShapeDtypeStruct((2 * width,...  16.9 us
    ppermute x12, starting transfers between devices, across(): return lax.ppermute(x, 'run', [(r, r ^ mask) for r in range(runs)])  16.8 us
    pallas_call x1, Pallas kernels, level1(): pl.pallas_call(level1_kernel, out_shape=jax.ShapeDtypeStruct((quarter, 2...  13.7 us
    all_to_all x1, starting transfers between devices, body(): lax.all_to_all(packed.reshape(shards, slots, width), 'space', 0, 0, tiled...  13 us
    all_to_all x1, waiting for transfers between devices, body(): lax.all_to_all(pieces, 'space', 0, 0, tiled=True, axis_index_groups=groups)  8.1 us
    ppermute x3, starting transfers between devices, other_core(): return lax.ppermute(x, 'space', [(s, s ^ 1) for s in range(shards)])  5.83 us
    all_to_all x1, waiting for transfers between devices, body(): lax.all_to_all(packed.reshape(shards, slots, width), 'space', 0, 0, tiled...  5.39 us
  transfers between devices with their start and end apart: 18, of which 11 were waited for; matrix products, arithmetic and copies ran while one was open for 4% of the time, Pallas kernels for 22%

profile of v1, /device:TPU:1, one launch (start us, length us, event | category | flops | bytes accessed | tf_op | source)
XLA Modules:
  0.0 153.3 jit_solution(17674566740326030331)
XLA Ops:
  0.7 1.3 broadcast_select_fusion.rows_ref
  2.0 2.2 %pack.1 = bf16[3072,256]{1,0:T(8,128)(2,1)} custom-call(s32[64]{0:T(128)S(1)} %dynamic-slice_bitcast_fusion.counts_ref, bf16[2048,256]{1,0:T(8,128)(2,1)S(1)} %broadcast_select_fusion.rows_ref), custom_call_target="tpu_custom_call" | custom-call | tf_op jit(solution)/shard_map/pack/pallas_call | solution.py:298
  4.2 13.0 %all-to-all-start = ((bf16[64,48,256]{2,1,0:T(8,128)(2,1)}), bf16[64,48,256]{2,1,0:T(8,128)(2,1)S(1)}, u32[]{:S(2)}, u32[]{:S(2)}) async-start(bf16[64,48,256]{2,1,0:T(8,128)(2,1)} %bitcast.2), calls=%async_computation | async-start | bytes 3145728 | tf_op jit(solution)/shard_map/all_to_all | solution.py:301
  17.2 2.8 %collective-permute-start.1 = (bf16[2048,256]{1,0:T(8,128)(2,1)S(1)}, bf16[2048,256]{1,0:T(8,128)(2,1)}, u32[]{:S(2)}, u32[]{:S(2)}) collective-permute-start(bf16[2048,256]{1,0:T(8,128)(2,1)S(1)} %broadcast_select_fusion.rows_ref), channel_id=1, source_target_pairs={{0,192},{64,128},{128,64},{192,0},{1,193},{65,129},{129,65},{193,1... | collective-permute-start | bytes 3145736 | tf_op jit(solution)/shard_map/ppermute | solution.py:286
  20.0 0.0 collective-permute-start
  20.0 0.5 fusion.4
  20.6 22.4 %collective-permute-done.1 = bf16[2048,256]{1,0:T(8,128)(2,1)} collective-permute-done((bf16[2048,256]{1,0:T(8,128)(2,1)S(1)}, bf16[2048,256]{1,0:T(8,128)(2,1)}, u32[]{:S(2)}, u32[]{:S(2)}) %collective-permute-start.1) | collective-permute-done | bytes 1048608 | tf_op jit(solution)/shard_map/ppermute | solution.py:286
  43.0 1.1 collective-permute-done
  44.1 1.8 %fusion = f32[256,256]{0,1:T(8,128)S(1)} fusion(bf16[2048,256]{1,0:T(8,128)(2,1)} %collective-permute-done.1, bf16[2048,256]{1,0:T(8,128)(2,1)S(1)} %broadcast_select_fusion.rows_ref, bf16[2048,256]{1,0:T(8,128)(2,1)} %collective-permute-done, pred[]{:T(512)S(6)} %lt.19), kind=kOutput, calls=%fused_computation | convolution fusion | flops 268959744 | bytes 3407873 | tf_op jit(solution)/shard_map/dot_general | solution.py:22
  45.9 1.7 %fusion.5 = f32[256,256]{0,1:T(8,128)S(1)} fusion(bf16[2048,256]{1,0:T(8,128)(2,1)S(1)} %broadcast_select_fusion.rows_ref, bf16[2048,256]{1,0:T(8,128)(2,1)} %collective-permute-done), kind=kOutput, calls=%fused_computation.22 | convolution fusion | flops 268435456 | bytes 2359296 | tf_op jit(solution)/shard_map/dot_general | solution.py:22
  47.7 1.7 %collective-permute-start.2 = (f32[256,384]{0,1:T(8,128)S(1)}, f32[256,384]{0,1:T(8,128)S(1)}, u32[]{:S(2)}, u32[]{:S(2)}) collective-permute-start(f32[256,384]{0,1:T(8,128)S(1)} %pad_maximum_fusion), channel_id=1, source_target_pairs={{0,1},{1,0},{2,3},{3,2},{4,5},{5,4},{6,7},{7,6},{8,9},{9,8},{10,11... | collective-permute-start | bytes 1179656 | tf_op jit(solution)/shard_map/ppermute | solution.py:289
  49.4 1.3 collective-permute-done.2
  50.7 0.1 maximum_add_fusion
  50.8 5.4 %all-to-all-done = bf16[64,48,256]{2,1,0:T(8,128)(2,1)S(1)} async-done(((bf16[64,48,256]{2,1,0:T(8,128)(2,1)}), bf16[64,48,256]{2,1,0:T(8,128)(2,1)S(1)}, u32[]{:S(2)}, u32[]{:S(2)}) %all-to-all-start) | async-done | bytes 1572896 | tf_op jit(solution)/shard_map/all_to_all | solution.py:301
  56.2 0.9 copy.4
  57.1 5.2 %all-to-all-start.1 = ((f32[32,8,384]{2,1,0:T(8,128)}), f32[32,8,384]{2,1,0:T(8,128)S(1)}, u32[]{:S(2)}, u32[]{:S(2)}) async-start(f32[32,8,384]{2,1,0:T(8,128)} %bitcast.3), calls=%async_computation.1 | async-start | bytes 786432 | tf_op jit(solution)/shard_map/all_to_all | solution.py:317
  62.3 0.2 dynamic-slice_reduce_fusion.counts_ref
  62.5 2.4 %unpack.1 = (bf16[2048,256]{1,0:T(8,128)(2,1)}, bf16[2048,256]{1,0:T(8,128)(2,1)}) custom-call(s32[64]{0:T(128)S(1)} %dynamic-slice_reduce_fusion.counts_ref, bf16[3072,256]{1,0:T(8,128)(2,1)S(1)} %bitcast.16), custom_call_target="tpu_custom_call" | custom-call | tf_op jit(solution)/shard_map/unpack/pallas_call | solution.py:313
  64.9 1.3 collective-permute-start.3
  66.2 1.9 %collective-permute-start.4 = (bf16[2048,256]{1,0:T(8,128)(2,1)}, bf16[2048,256]{1,0:T(8,128)(2,1)S(1)}, u32[]{:S(2)}, u32[]{:S(2)}) collective-permute-start(bf16[2048,256]{1,0:T(8,128)(2,1)} %get-tuple-element.32), channel_id=1, source_target_pairs={{0,192},{64,128},{128,64},{192,0},{1,193},{65,129},{129,65},{193,1... | collective-permute-start | bytes 3145736 | tf_op jit(solution)/shard_map/ppermute | solution.py:286
  68.1 8.1 %all-to-all-done.1 = f32[32,8,384]{2,1,0:T(8,128)S(1)} async-done(((f32[32,8,384]{2,1,0:T(8,128)}), f32[32,8,384]{2,1,0:T(8,128)S(1)}, u32[]{:S(2)}, u32[]{:S(2)}) %all-to-all-start.1) | async-done | bytes 393248 | tf_op jit(solution)/shard_map/all_to_all | solution.py:317
  76.3 0.8 broadcast_in_dim.18
  77.0 4.9 %all-to-all-start.2 = ((f32[32,8,384]{2,1,0:T(8,128)}), f32[32,8,384]{2,1,0:T(8,128)S(1)}, u32[]{:S(2)}, u32[]{:S(2)}) async-start(f32[32,8,384]{2,1,0:T(8,128)} %broadcast_in_dim.18), calls=%async_computation.2 | async-start | bytes 786432 | tf_op jit(solution)/shard_map/all_to_all | solution.py:321
  81.9 6.8 %collective-permute-done.3.p1 = bf16[2048,256]{1,0:T(8,128)(2,1)S(1)} collective-permute-done((bf16[2048,256]{1,0:T(8,128)(2,1)}, bf16[2048,256]{1,0:T(8,128)(2,1)S(1)}, u32[]{:S(2)}, u32[]{:S(2)}) %collective-permute-start.3) | collective-permute-done | bytes 1048608 | tf_op jit(solution)/shard_map/ppermute | solution.py:286
  88.8 2.2 %collective-permute-done.4.p3 = bf16[2048,256]{1,0:T(8,128)(2,1)S(1)} collective-permute-done((bf16[2048,256]{1,0:T(8,128)(2,1)}, bf16[2048,256]{1,0:T(8,128)(2,1)S(1)}, u32[]{:S(2)}, u32[]{:S(2)}) %collective-permute-start.4) | collective-permute-done | bytes 1048608 | tf_op jit(solution)/shard_map/ppermute | solution.py:286
  90.9 0.8 slice.64
  91.8 3.0 %all-to-all-done.2 = f32[32,8,384]{2,1,0:T(8,128)S(1)} async-done(((f32[32,8,384]{2,1,0:T(8,128)}), f32[32,8,384]{2,1,0:T(8,128)S(1)}, u32[]{:S(2)}, u32[]{:S(2)}) %all-to-all-start.2) | async-done | bytes 393248 | tf_op jit(solution)/shard_map/all_to_all | solution.py:321
  94.8 3.3 %collective-permute-start.8 = (f32[256,384]{1,0:T(8,128)S(1)}, f32[256,384]{1,0:T(8,128)S(1)}, u32[]{:S(2)}, u32[]{:S(2)}) collective-permute-start(f32[256,384]{1,0:T(8,128)S(1)} %bitcast.17), channel_id=1, source_target_pairs={{0,1},{1,0},{2,3},{3,2},{4,5},{5,4},{6,7},{7,6},{8,9},{9,8},{10,11... | collective-permute-start | bytes 1179656 | tf_op jit(solution)/shard_map/ppermute | solution.py:289
  98.2 2.8 %collective-permute-start.7 = (f32[256,256]{1,0:T(8,128)S(1)}, f32[256,256]{1,0:T(8,128)S(1)}, u32[]{:S(2)}, u32[]{:S(2)}) collective-permute-start(f32[256,256]{1,0:T(8,128)S(1)} %slice.54), channel_id=1, source_target_pairs={{0,192},{64,128},{128,64},{192,0},{1,193},{65,129},{129,65},{193,1... | collective-permute-start | bytes 786440 | tf_op jit(solution)/shard_map/ppermute | solution.py:286
  101.0 0.1 collective-permute-start.5
  101.1 1.2 collective-permute-start.6
  102.3 0.0 collective-permute-done.8.refs_1_
  102.4 3.6 %collective-permute-done.5 = f32[256,128]{1,0:T(8,128)S(1)} collective-permute-done((f32[256,128]{1,0:T(8,128)S(1)}, f32[256,128]{1,0:T(8,128)S(1)}, u32[]{:S(2)}, u32[]{:S(2)}) %collective-permute-start.5) | collective-permute-done | bytes 131104 | tf_op jit(solution)/shard_map/ppermute | solution.py:286
  105.9 2.7 %collective-permute-done.6 = f32[256,128]{1,0:T(8,128)S(1)} collective-permute-done((f32[256,128]{1,0:T(8,128)S(1)}, f32[256,128]{1,0:T(8,128)S(1)}, u32[]{:S(2)}, u32[]{:S(2)}) %collective-permute-start.6) | collective-permute-done | bytes 131104 | tf_op jit(solution)/shard_map/ppermute | solution.py:286
  108.6 1.8 %collective-permute-done.7 = f32[256,256]{1,0:T(8,128)S(1)} collective-permute-done((f32[256,256]{1,0:T(8,128)S(1)}, f32[256,256]{1,0:T(8,128)S(1)}, u32[]{:S(2)}, u32[]{:S(2)}) %collective-permute-start.7) | collective-permute-done | bytes 262176 | tf_op jit(solution)/shard_map/ppermute | solution.py:286
  110.4 0.8 collective-permute-start.9
  111.2 0.1 pad_add_fusion.place_ref
  111.3 0.0 collective-permute-start.12
  111.4 3.8 %collective-permute-start.13 = (f32[256,256]{1,0:T(8,128)S(1)}, f32[256,256]{1,0:T(8,128)S(1)}, u32[]{:S(2)}, u32[]{:S(2)}) collective-permute-start(f32[256,256]{1,0:T(8,128)S(1)} %maximum_select_fusion.c0_ref), channel_id=1, source_target_pairs={{0,128},{64,192},{128,0},{192,64},{1,129},{65,193},{129,1},{193,65... | collective-permute-start | bytes 786440 | tf_op jit(solution)/shard_map/ppermute | solution.py:286
  115.2 0.0 collective-permute-start.14
  115.2 16.9 %level0.1 = (bf16[512,256]{1,0:T(8,128)(2,1)S(1)}, bf16[512,256]{1,0:T(8,128)(2,1)S(1)}, f32[2,256,256]{2,1,0:T(8,128)S(1)}) custom-call(s32[2]{0:T(128)S(1)} %pad_add_fusion.place_ref, f32[256,384]{1,0:T(8,128)S(1)} %bitcast.20, f32[256,384]{1,0:T(8,128)S(1)} %collective-permute-done.8.refs_1_, f32[256,512]{1,0:T(8,128)S(1)} %constant_dynamic-update-slice_fusion.refs_2_, ...), custom_call_target="tpu_custom_call" | custom-call | flops 12000000000 | bytes 2097152 | tf_op jit(solution)/shard_map/level0/pallas_call | solution.py:124
  132.1 2.8 %collective-permute-start.10 = (bf16[1024,256]{1,0:T(8,128)(2,1)S(1)}, bf16[1024,256]{1,0:T(8,128)(2,1)S(1)}, u32[]{:S(2)}, u32[]{:S(2)}) collective-permute-start(bf16[1024,256]{1,0:T(8,128)(2,1)S(1)} %slice.63), channel_id=1, source_target_pairs={{0,192},{64,128},{128,64},{192,0},{1,193},{65,129},{129,65},{193,1... | collective-permute-start | bytes 1572872 | tf_op jit(solution)/shard_map/ppermute | solution.py:286
  134.9 0.0 collective-permute-start.11
  134.9 0.0 collective-permute-done.12.c1_ref
  134.9 0.0 collective-permute-done.14.c3_ref
  134.9 13.7 %level1.1.last_ref = bf16[64,512]{1,0:T(8,128)(2,1)S(1)} custom-call(s32[2]{0:T(128)S(1)} %pad_add_fusion.place_ref, bf16[512,256]{1,0:T(8,128)(2,1)S(1)} %get-tuple-element.45.near_ref, bf16[512,256]{1,0:T(8,128)(2,1)S(1)} %get-tuple-element.46.far_ref, f32[2,256,256]{2,1,0:T(8,128)S(1)} %get-tuple-element.47.outer_ref, ...), custom_call_target="tpu_custom_call" | custom-call | flops 8000000000 | bytes 2097152 | tf_op jit(solution)/shard_map/level1/pallas_call | solution.py:174
  148.7 0.0 collective-permute-done.11.p2b
  148.7 4.6 %rotate.1 = bf16[64,2048]{1,0:T(8,128)(2,1)} custom-call(bf16[2048,256]{1,0:T(8,128)(2,1)} %get-tuple-element.30.own, bf16[2048,256]{1,0:T(8,128)(2,1)S(1)} %collective-permute-done.3.p1, bf16[1024,256]{1,0:T(8,128)(2,1)S(1)} %collective-permute-done.10.p2a, bf16[1024,256]{1,0:T(8,128)(2,1)S(1)} %collective-permute-done.11.p2b, ...), custom_call_target="tpu_custom_call" | custom-call | tf_op jit(solution)/shard_map/rotate/pallas_call | solution.py:251
  (22 shorter events, 0.3 us)
Async XLA Ops:
  0.0 2.0 %copy-start = (s32[64,64]{1,0:T(8,128)S(1)}, s32[64,64]{1,0:T(8,128)}, u32[]{:S(2)}) copy-start(s32[64,64]{1,0:T(8,128)} %param.5) | copy-start | bytes 49156
  4.2 52.0 %all-to-all-start = ((bf16[64,48,256]{2,1,0:T(8,128)(2,1)}), bf16[64,48,256]{2,1,0:T(8,128)(2,1)S(1)}, u32[]{:S(2)}, u32[]{:S(2)}) async-start(bf16[64,48,256]{2,1,0:T(8,128)(2,1)} %bitcast.2), calls=%async_computation | async-start | bytes 3145728 | tf_op jit(solution)/shard_map/all_to_all | solution.py:301
  17.2 25.8 %collective-permute-start.1 = (bf16[2048,256]{1,0:T(8,128)(2,1)S(1)}, bf16[2048,256]{1,0:T(8,128)(2,1)}, u32[]{:S(2)}, u32[]{:S(2)}) collective-permute-start(bf16[2048,256]{1,0:T(8,128)(2,1)S(1)} %broadcast_select_fusion.rows_ref), channel_id=1, source_target_pairs={{0,192},{64,128},{128,64},{192,0},{1,193},{65,129},{129,65},{193,1... | collective-permute-start | bytes 3145736 | tf_op jit(solution)/shard_map/ppermute | solution.py:286
  20.0 24.1 %collective-permute-start = (bf16[2048,256]{1,0:T(8,128)(2,1)S(1)}, bf16[2048,256]{1,0:T(8,128)(2,1)}, u32[]{:S(2)}, u32[]{:S(2)}) collective-permute-start(bf16[2048,256]{1,0:T(8,128)(2,1)S(1)} %broadcast_select_fusion.rows_ref), channel_id=1, source_target_pairs={{0,64},{64,0},{128,192},{192,128},{1,65},{65,1},{129,193},{193,129... | collective-permute-start | bytes 3145736 | tf_op jit(solution)/shard_map/ppermute | solution.py:286
  47.7 3.1 %collective-permute-start.2 = (f32[256,384]{0,1:T(8,128)S(1)}, f32[256,384]{0,1:T(8,128)S(1)}, u32[]{:S(2)}, u32[]{:S(2)}) collective-permute-start(f32[256,384]{0,1:T(8,128)S(1)} %pad_maximum_fusion), channel_id=1, source_target_pairs={{0,1},{1,0},{2,3},{3,2},{4,5},{5,4},{6,7},{7,6},{8,9},{9,8},{10,11... | collective-permute-start | bytes 1179656 | tf_op jit(solution)/shard_map/ppermute | solution.py:289
  57.1 19.1 %all-to-all-start.1 = ((f32[32,8,384]{2,1,0:T(8,128)}), f32[32,8,384]{2,1,0:T(8,128)S(1)}, u32[]{:S(2)}, u32[]{:S(2)}) async-start(f32[32,8,384]{2,1,0:T(8,128)} %bitcast.3), calls=%async_computation.1 | async-start | bytes 786432 | tf_op jit(solution)/shard_map/all_to_all | solution.py:317
  64.9 23.8 %collective-permute-start.3 = (bf16[2048,256]{1,0:T(8,128)(2,1)}, bf16[2048,256]{1,0:T(8,128)(2,1)S(1)}, u32[]{:S(2)}, u32[]{:S(2)}) collective-permute-start(bf16[2048,256]{1,0:T(8,128)(2,1)} %get-tuple-element.30.own), channel_id=1, source_target_pairs={{0,64},{64,0},{128,192},{192,128},{1,65},{65,1},{129,193},{193,129... | collective-permute-start | bytes 3145736 | tf_op jit(solution)/shard_map/ppermute | solution.py:286
  66.2 24.7 %collective-permute-start.4 = (bf16[2048,256]{1,0:T(8,128)(2,1)}, bf16[2048,256]{1,0:T(8,128)(2,1)S(1)}, u32[]{:S(2)}, u32[]{:S(2)}) collective-permute-start(bf16[2048,256]{1,0:T(8,128)(2,1)} %get-tuple-element.32), channel_id=1, source_target_pairs={{0,192},{64,128},{128,64},{192,0},{1,193},{65,129},{129,65},{193,1... | collective-permute-start | bytes 3145736 | tf_op jit(solution)/shard_map/ppermute | solution.py:286
  77.0 17.8 %all-to-all-start.2 = ((f32[32,8,384]{2,1,0:T(8,128)}), f32[32,8,384]{2,1,0:T(8,128)S(1)}, u32[]{:S(2)}, u32[]{:S(2)}) async-start(f32[32,8,384]{2,1,0:T(8,128)} %broadcast_in_dim.18), calls=%async_computation.2 | async-start | bytes 786432 | tf_op jit(solution)/shard_map/all_to_all | solution.py:321
  94.8 7.5 %collective-permute-start.8 = (f32[256,384]{1,0:T(8,128)S(1)}, f32[256,384]{1,0:T(8,128)S(1)}, u32[]{:S(2)}, u32[]{:S(2)}) collective-permute-start(f32[256,384]{1,0:T(8,128)S(1)} %bitcast.17), channel_id=1, source_target_pairs={{0,1},{1,0},{2,3},{3,2},{4,5},{5,4},{6,7},{7,6},{8,9},{9,8},{10,11... | collective-permute-start | bytes 1179656 | tf_op jit(solution)/shard_map/ppermute | solution.py:289
  98.2 12.2 %collective-permute-start.7 = (f32[256,256]{1,0:T(8,128)S(1)}, f32[256,256]{1,0:T(8,128)S(1)}, u32[]{:S(2)}, u32[]{:S(2)}) collective-permute-start(f32[256,256]{1,0:T(8,128)S(1)} %slice.54), channel_id=1, source_target_pairs={{0,192},{64,128},{128,64},{192,0},{1,193},{65,129},{129,65},{193,1... | collective-permute-start | bytes 786440 | tf_op jit(solution)/shard_map/ppermute | solution.py:286
  101.0 4.9 %collective-permute-start.5 = (f32[256,128]{1,0:T(8,128)S(1)}, f32[256,128]{1,0:T(8,128)S(1)}, u32[]{:S(2)}, u32[]{:S(2)}) collective-permute-start(f32[256,128]{1,0:T(8,128)S(1)} %get-tuple-element.50), channel_id=1, source_target_pairs={{0,64},{64,0},{128,192},{192,128},{1,65},{65,1},{129,193},{193,129... | collective-permute-start | bytes 393224 | tf_op jit(solution)/shard_map/ppermute | solution.py:286
  101.1 7.5 %collective-permute-start.6 = (f32[256,128]{1,0:T(8,128)S(1)}, f32[256,128]{1,0:T(8,128)S(1)}, u32[]{:S(2)}, u32[]{:S(2)}) collective-permute-start(f32[256,128]{1,0:T(8,128)S(1)} %get-tuple-element.50), channel_id=1, source_target_pairs={{0,128},{64,192},{128,0},{192,64},{1,129},{65,193},{129,1},{193,65... | collective-permute-start | bytes 393224 | tf_op jit(solution)/shard_map/ppermute | solution.py:286
  110.4 4.8 %collective-permute-start.9 = (f32[256,512]{1,0:T(8,128)S(1)}, f32[256,512]{1,0:T(8,128)S(1)}, u32[]{:S(2)}, u32[]{:S(2)}) collective-permute-start(f32[256,512]{1,0:T(8,128)S(1)} %constant_dynamic-update-slice_fusion.refs_2_), channel_id=1, source_target_pairs={{0,1},{1,0},{2,3},{3,2},{4,5},{5,4},{6,7},{7,6},{8,9},{9,8},{10,11... | collective-permute-start | bytes 1572872 | tf_op jit(solution)/shard_map/ppermute | solution.py:289
  111.3 23.6 %copy-start.1 = (bf16[1024,256]{1,0:T(8,128)(2,1)S(1)}, bf16[1024,256]{1,0:T(8,128)(2,1)}, u32[]{:S(2)}) copy-start(bf16[1024,256]{1,0:T(8,128)(2,1)} %slice.64) | copy-start | bytes 1572868
  111.3 23.6 %collective-permute-start.12 = (f32[256,256]{1,0:T(8,128)S(1)}, f32[256,256]{1,0:T(8,128)S(1)}, u32[]{:S(2)}, u32[]{:S(2)}) collective-permute-start(f32[256,256]{1,0:T(8,128)S(1)} %maximum_select_fusion.c0_ref), channel_id=1, source_target_pairs={{0,64},{64,0},{128,192},{192,128},{1,65},{65,1},{129,193},{193,129... | collective-permute-start | bytes 786440 | tf_op jit(solution)/shard_map/ppermute | solution.py:286
  111.4 23.6 %collective-permute-start.13 = (f32[256,256]{1,0:T(8,128)S(1)}, f32[256,256]{1,0:T(8,128)S(1)}, u32[]{:S(2)}, u32[]{:S(2)}) collective-permute-start(f32[256,256]{1,0:T(8,128)S(1)} %maximum_select_fusion.c0_ref), channel_id=1, source_target_pairs={{0,128},{64,192},{128,0},{192,64},{1,129},{65,193},{129,1},{193,65... | collective-permute-start | bytes 786440 | tf_op jit(solution)/shard_map/ppermute | solution.py:286
  115.2 19.7 %collective-permute-start.14 = (f32[256,256]{1,0:T(8,128)S(1)}, f32[256,256]{1,0:T(8,128)S(1)}, u32[]{:S(2)}, u32[]{:S(2)}) collective-permute-start(f32[256,256]{1,0:T(8,128)S(1)} %maximum_select_fusion.c0_ref), channel_id=1, source_target_pairs={{0,192},{64,128},{128,64},{192,0},{1,193},{65,129},{129,65},{193,1... | collective-permute-start | bytes 786440 | tf_op jit(solution)/shard_map/ppermute | solution.py:286
  132.1 16.5 %collective-permute-start.10 = (bf16[1024,256]{1,0:T(8,128)(2,1)S(1)}, bf16[1024,256]{1,0:T(8,128)(2,1)S(1)}, u32[]{:S(2)}, u32[]{:S(2)}) collective-permute-start(bf16[1024,256]{1,0:T(8,128)(2,1)S(1)} %slice.63), channel_id=1, source_target_pairs={{0,192},{64,128},{128,64},{192,0},{1,193},{65,129},{129,65},{193,1... | collective-permute-start | bytes 1572872 | tf_op jit(solution)/shard_map/ppermute | solution.py:286
  134.9 13.8 %collective-permute-start.11 = (bf16[1024,256]{1,0:T(8,128)(2,1)S(1)}, bf16[1024,256]{1,0:T(8,128)(2,1)S(1)}, u32[]{:S(2)}, u32[]{:S(2)}) collective-permute-start(bf16[1024,256]{1,0:T(8,128)(2,1)S(1)} %copy-done.1), channel_id=1, source_target_pairs={{0,64},{64,0},{128,192},{192,128},{1,65},{65,1},{129,193},{193,129... | collective-permute-start | bytes 1572872 | tf_op jit(solution)/shard_map/ppermute | solution.py:286

commit v2 on v1

--- a/solution.py
+++ b/solution.py
@@ -221,39 +221,39 @@
             turned_ref[pl.ds((1 - k) * half, half), at] = rows
 
 
-def rotate_kernel(tiles, own, p1, p2a, p2b, p3, near_ref, far_ref, last_ref, out_ref):
-    width = near_ref.shape[1]
-
-    def turn(p2):
-        near = (dot(own[...], near_ref[:width]) + dot(p1[...], near_ref[width:])).astype(BF)
-        far = (dot(p3[...], far_ref[:width]) + dot(p2[...], far_ref[width:])).astype(BF)
+def rotate_kernel(own, p1, p2a, p2b, p3, near_ref, far_ref, last_ref, out_ref):
+    step, steps = pl.program_id(0), pl.num_programs(0)
+    cells, width = own.shape
+    tile = out_ref.shape[1]
+    half = cells // 2
+    first = pl.multiple_of(step * tile, tile)
+
+    def turn(p2, inside, other):
+        at = pl.ds(first, tile)
+        near = (dot(own[at], near_ref[:width]) + dot(p1[at], near_ref[width:])).astype(BF)
+        rows = p2[pl.ds(pl.multiple_of(inside, tile), tile)]
+        mate = p3[pl.ds(pl.multiple_of(other, tile), tile)]
+        far = (dot(mate, far_ref[:width]) + dot(rows, far_ref[width:])).astype(BF)
         out_ref[...] = (dot_nt(last_ref[:, :width], near) + dot_nt(last_ref[:, width:], far)).astype(BF)
 
-    @pl.when(pl.program_id(0) < tiles)
+    @pl.when(step < steps // 2)
     def _():
-        turn(p2a)
-
-    @pl.when(pl.program_id(0) >= tiles)
+        turn(p2a, first, first + half)
+
+    @pl.when(step >= steps // 2)
     def _():
-        turn(p2b)
+        turn(p2b, first - half, first - half)
 
 
 def rotate(own, p1, p2a, p2b, p3, near, far, last):
-    quarter = last.shape[0]
-    tiles = 2
-    cells, width = own.shape
-    tile = cells // (2 * tiles)
-    straight = pl.BlockSpec((tile, width), lambda i: (i, 0))
-    low = pl.BlockSpec((tile, width), lambda i: (jnp.minimum(i, tiles - 1), 0))
-    high = pl.BlockSpec((tile, width), lambda i: (jnp.maximum(i - tiles, 0), 0))
-    swapped = pl.BlockSpec((tile, width), lambda i: (jnp.where(i < tiles, i + tiles, i - tiles), 0))
-    whole = [pl.BlockSpec(x.shape, lambda i: (0, 0)) for x in (near, far, last)]
+    quarter, steps = last.shape[0], 4
+    cells = own.shape[0]
     return pl.pallas_call(
-        functools.partial(rotate_kernel, tiles),
-        grid=(2 * tiles,),
+        rotate_kernel,
+        grid=(steps,),
         out_shape=jax.ShapeDtypeStruct((quarter, cells), BF),
-        in_specs=[straight, straight, low, high, swapped] + whole,
-        out_specs=pl.BlockSpec((quarter, tile), lambda i: (0, i)),
+        in_specs=[pl.BlockSpec(memory_space=pltpu.VMEM)] * 8,
+        out_specs=pl.BlockSpec((quarter, cells // steps), lambda i: (0, i)),
         compiler_params=pltpu.CompilerParams(vmem_limit_bytes=40 * 2**20),
         name="rotate",
     )(own, p1, p2a, p2b, p3, near, far, last)

time: 154 us -> 154 us (level)
  no operation moved by 1% of the time
where the time goes in v2:
time: 154 us; the launch traced here: 153 us
  waiting for transfers between devices  58.4 us (38%)
  starting transfers between devices  45.7 us (30%)
  Pallas kernels  39.9 us (26%)
  matrix products  4.02 us (3%)
  local copies, waits for them, and re-layouts  2.84 us (2%)
  other arithmetic  1.59 us (1%)
    ppermute x12, waiting for transfers between devices, across(): return lax.ppermute(x, 'run', [(r, r ^ mask) for r in range(runs)])  40.5 us
    pallas_call x1, Pallas kernels, level0(): pl.pallas_call(level0_kernel, out_shape=[jax.ShapeDtypeStruct((2 * width,...  16.9 us
    ppermute x12, starting transfers between devices, across(): return lax.ppermute(x, 'run', [(r, r ^ mask) for r in range(runs)])  16.8 us
    pallas_call x1, Pallas kernels, level1(): pl.pallas_call(level1_kernel, out_shape=jax.ShapeDtypeStruct((quarter, 2...  13.7 us
    all_to_all x1, starting transfers between devices, body(): lax.all_to_all(packed.reshape(shards, slots, width), 'space', 0, 0, tiled...  13 us
    all_to_all x1, waiting for transfers between devices, body(): lax.all_to_all(pieces, 'space', 0, 0, tiled=True, axis_index_groups=groups)  8.1 us
    ppermute x3, starting transfers between devices, other_core(): return lax.ppermute(x, 'space', [(s, s ^ 1) for s in range(shards)])  5.83 us
    all_to_all x1, waiting for transfers between devices, body(): lax.all_to_all(packed.reshape(shards, slots, width), 'space', 0, 0, tiled...  5.39 us
  transfers between devices with their start and end apart: 18, of which 11 were waited for; matrix products, arithmetic and copies ran while one was open for 4% of the time, Pallas kernels for 22%

profile of v2, /device:TPU:1, one launch (start us, length us, event | category | flops | bytes accessed | tf_op | source)
XLA Modules:
  0.0 153.3 jit_solution(11296582678264031335)
XLA Ops:
  0.7 1.3 broadcast_select_fusion.rows_ref
  2.0 2.2 %pack.1 = bf16[3072,256]{1,0:T(8,128)(2,1)} custom-call(s32[64]{0:T(128)S(1)} %dynamic-slice_bitcast_fusion.counts_ref, bf16[2048,256]{1,0:T(8,128)(2,1)S(1)} %broadcast_select_fusion.rows_ref), custom_call_target="tpu_custom_call" | custom-call | tf_op jit(solution)/shard_map/pack/pallas_call | solution.py:298
  4.2 13.0 %all-to-all-start = ((bf16[64,48,256]{2,1,0:T(8,128)(2,1)}), bf16[64,48,256]{2,1,0:T(8,128)(2,1)S(1)}, u32[]{:S(2)}, u32[]{:S(2)}) async-start(bf16[64,48,256]{2,1,0:T(8,128)(2,1)} %bitcast.2), calls=%async_computation | async-start | bytes 3145728 | tf_op jit(solution)/shard_map/all_to_all | solution.py:301
  17.2 2.8 %collective-permute-start.1 = (bf16[2048,256]{1,0:T(8,128)(2,1)S(1)}, bf16[2048,256]{1,0:T(8,128)(2,1)}, u32[]{:S(2)}, u32[]{:S(2)}) collective-permute-start(bf16[2048,256]{1,0:T(8,128)(2,1)S(1)} %broadcast_select_fusion.rows_ref), channel_id=1, source_target_pairs={{0,192},{64,128},{128,64},{192,0},{1,193},{65,129},{129,65},{193,1... | collective-permute-start | bytes 3145736 | tf_op jit(solution)/shard_map/ppermute | solution.py:286
  20.0 0.0 collective-permute-start
  20.0 0.5 fusion.4
  20.6 22.4 %collective-permute-done.1 = bf16[2048,256]{1,0:T(8,128)(2,1)} collective-permute-done((bf16[2048,256]{1,0:T(8,128)(2,1)S(1)}, bf16[2048,256]{1,0:T(8,128)(2,1)}, u32[]{:S(2)}, u32[]{:S(2)}) %collective-permute-start.1) | collective-permute-done | bytes 1048608 | tf_op jit(solution)/shard_map/ppermute | solution.py:286
  43.0 1.1 collective-permute-done
  44.1 1.8 %fusion = f32[256,256]{0,1:T(8,128)S(1)} fusion(bf16[2048,256]{1,0:T(8,128)(2,1)} %collective-permute-done.1, bf16[2048,256]{1,0:T(8,128)(2,1)S(1)} %broadcast_select_fusion.rows_ref, bf16[2048,256]{1,0:T(8,128)(2,1)} %collective-permute-done, pred[]{:T(512)S(6)} %lt.19), kind=kOutput, calls=%fused_computation | convolution fusion | flops 268959744 | bytes 3407873 | tf_op jit(solution)/shard_map/dot_general | solution.py:22
  45.9 1.7 %fusion.5 = f32[256,256]{0,1:T(8,128)S(1)} fusion(bf16[2048,256]{1,0:T(8,128)(2,1)S(1)} %broadcast_select_fusion.rows_ref, bf16[2048,256]{1,0:T(8,128)(2,1)} %collective-permute-done), kind=kOutput, calls=%fused_computation.22 | convolution fusion | flops 268435456 | bytes 2359296 | tf_op jit(solution)/shard_map/dot_general | solution.py:22
  47.7 1.7 %collective-permute-start.2 = (f32[256,384]{0,1:T(8,128)S(1)}, f32[256,384]{0,1:T(8,128)S(1)}, u32[]{:S(2)}, u32[]{:S(2)}) collective-permute-start(f32[256,384]{0,1:T(8,128)S(1)} %pad_maximum_fusion), channel_id=1, source_target_pairs={{0,1},{1,0},{2,3},{3,2},{4,5},{5,4},{6,7},{7,6},{8,9},{9,8},{10,11... | collective-permute-start | bytes 1179656 | tf_op jit(solution)/shard_map/ppermute | solution.py:289
  49.4 1.3 collective-permute-done.2
  50.7 0.1 maximum_add_fusion
  50.8 5.4 %all-to-all-done = bf16[64,48,256]{2,1,0:T(8,128)(2,1)S(1)} async-done(((bf16[64,48,256]{2,1,0:T(8,128)(2,1)}), bf16[64,48,256]{2,1,0:T(8,128)(2,1)S(1)}, u32[]{:S(2)}, u32[]{:S(2)}) %all-to-all-start) | async-done | bytes 1572896 | tf_op jit(solution)/shard_map/all_to_all | solution.py:301
  56.2 0.9 copy.4
  57.1 5.2 %all-to-all-start.1 = ((f32[32,8,384]{2,1,0:T(8,128)}), f32[32,8,384]{2,1,0:T(8,128)S(1)}, u32[]{:S(2)}, u32[]{:S(2)}) async-start(f32[32,8,384]{2,1,0:T(8,128)} %bitcast.3), calls=%async_computation.1 | async-start | bytes 786432 | tf_op jit(solution)/shard_map/all_to_all | solution.py:317
  62.3 0.2 dynamic-slice_reduce_fusion.counts_ref
  62.5 2.4 %unpack.1 = (bf16[2048,256]{1,0:T(8,128)(2,1)}, bf16[2048,256]{1,0:T(8,128)(2,1)}) custom-call(s32[64]{0:T(128)S(1)} %dynamic-slice_reduce_fusion.counts_ref, bf16[3072,256]{1,0:T(8,128)(2,1)S(1)} %bitcast.16), custom_call_target="tpu_custom_call" | custom-call | tf_op jit(solution)/shard_map/unpack/pallas_call | solution.py:313
  64.9 1.3 collective-permute-start.3
  66.2 1.9 %collective-permute-start.4 = (bf16[2048,256]{1,0:T(8,128)(2,1)}, bf16[2048,256]{1,0:T(8,128)(2,1)S(1)}, u32[]{:S(2)}, u32[]{:S(2)}) collective-permute-start(bf16[2048,256]{1,0:T(8,128)(2,1)} %get-tuple-element.32), channel_id=1, source_target_pairs={{0,192},{64,128},{128,64},{192,0},{1,193},{65,129},{129,65},{193,1... | collective-permute-start | bytes 3145736 | tf_op jit(solution)/shard_map/ppermute | solution.py:286
  68.1 8.1 %all-to-all-done.1 = f32[32,8,384]{2,1,0:T(8,128)S(1)} async-done(((f32[32,8,384]{2,1,0:T(8,128)}), f32[32,8,384]{2,1,0:T(8,128)S(1)}, u32[]{:S(2)}, u32[]{:S(2)}) %all-to-all-start.1) | async-done | bytes 393248 | tf_op jit(solution)/shard_map/all_to_all | solution.py:317
  76.3 0.8 broadcast_in_dim.18
  77.0 4.9 %all-to-all-start.2 = ((f32[32,8,384]{2,1,0:T(8,128)}), f32[32,8,384]{2,1,0:T(8,128)S(1)}, u32[]{:S(2)}, u32[]{:S(2)}) async-start(f32[32,8,384]{2,1,0:T(8,128)} %broadcast_in_dim.18), calls=%async_computation.2 | async-start | bytes 786432 | tf_op jit(solution)/shard_map/all_to_all | solution.py:321
  81.9 6.8 %collective-permute-done.3.p1 = bf16[2048,256]{1,0:T(8,128)(2,1)S(1)} collective-permute-done((bf16[2048,256]{1,0:T(8,128)(2,1)}, bf16[2048,256]{1,0:T(8,128)(2,1)S(1)}, u32[]{:S(2)}, u32[]{:S(2)}) %collective-permute-start.3) | collective-permute-done | bytes 1048608 | tf_op jit(solution)/shard_map/ppermute | solution.py:286
  88.8 2.2 %collective-permute-done.4.p3 = bf16[2048,256]{1,0:T(8,128)(2,1)S(1)} collective-permute-done((bf16[2048,256]{1,0:T(8,128)(2,1)}, bf16[2048,256]{1,0:T(8,128)(2,1)S(1)}, u32[]{:S(2)}, u32[]{:S(2)}) %collective-permute-start.4) | collective-permute-done | bytes 1048608 | tf_op jit(solution)/shard_map/ppermute | solution.py:286
  90.9 0.8 slice.64
  91.8 3.0 %all-to-all-done.2 = f32[32,8,384]{2,1,0:T(8,128)S(1)} async-done(((f32[32,8,384]{2,1,0:T(8,128)}), f32[32,8,384]{2,1,0:T(8,128)S(1)}, u32[]{:S(2)}, u32[]{:S(2)}) %all-to-all-start.2) | async-done | bytes 393248 | tf_op jit(solution)/shard_map/all_to_all | solution.py:321
  94.8 3.3 %collective-permute-start.8 = (f32[256,384]{1,0:T(8,128)S(1)}, f32[256,384]{1,0:T(8,128)S(1)}, u32[]{:S(2)}, u32[]{:S(2)}) collective-permute-start(f32[256,384]{1,0:T(8,128)S(1)} %bitcast.17), channel_id=1, source_target_pairs={{0,1},{1,0},{2,3},{3,2},{4,5},{5,4},{6,7},{7,6},{8,9},{9,8},{10,11... | collective-permute-start | bytes 1179656 | tf_op jit(solution)/shard_map/ppermute | solution.py:289
  98.2 2.8 %collective-permute-start.7 = (f32[256,256]{1,0:T(8,128)S(1)}, f32[256,256]{1,0:T(8,128)S(1)}, u32[]{:S(2)}, u32[]{:S(2)}) collective-permute-start(f32[256,256]{1,0:T(8,128)S(1)} %slice.54), channel_id=1, source_target_pairs={{0,192},{64,128},{128,64},{192,0},{1,193},{65,129},{129,65},{193,1... | collective-permute-start | bytes 786440 | tf_op jit(solution)/shard_map/ppermute | solution.py:286
  101.0 0.1 collective-permute-start.5
  101.1 1.2 collective-permute-start.6
  102.3 0.0 collective-permute-done.8.refs_1_
  102.4 3.6 %collective-permute-done.5 = f32[256,128]{1,0:T(8,128)S(1)} collective-permute-done((f32[256,128]{1,0:T(8,128)S(1)}, f32[256,128]{1,0:T(8,128)S(1)}, u32[]{:S(2)}, u32[]{:S(2)}) %collective-permute-start.5) | collective-permute-done | bytes 131104 | tf_op jit(solution)/shard_map/ppermute | solution.py:286
  105.9 2.7 %collective-permute-done.6 = f32[256,128]{1,0:T(8,128)S(1)} collective-permute-done((f32[256,128]{1,0:T(8,128)S(1)}, f32[256,128]{1,0:T(8,128)S(1)}, u32[]{:S(2)}, u32[]{:S(2)}) %collective-permute-start.6) | collective-permute-done | bytes 131104 | tf_op jit(solution)/shard_map/ppermute | solution.py:286
  108.6 1.8 %collective-permute-done.7 = f32[256,256]{1,0:T(8,128)S(1)} collective-permute-done((f32[256,256]{1,0:T(8,128)S(1)}, f32[256,256]{1,0:T(8,128)S(1)}, u32[]{:S(2)}, u32[]{:S(2)}) %collective-permute-start.7) | collective-permute-done | bytes 262176 | tf_op jit(solution)/shard_map/ppermute | solution.py:286
  110.4 0.8 collective-permute-start.9
  111.2 0.1 pad_add_fusion.place_ref
  111.3 0.0 collective-permute-start.12
  111.4 3.8 %collective-permute-start.13 = (f32[256,256]{1,0:T(8,128)S(1)}, f32[256,256]{1,0:T(8,128)S(1)}, u32[]{:S(2)}, u32[]{:S(2)}) collective-permute-start(f32[256,256]{1,0:T(8,128)S(1)} %maximum_select_fusion.c0_ref), channel_id=1, source_target_pairs={{0,128},{64,192},{128,0},{192,64},{1,129},{65,193},{129,1},{193,65... | collective-permute-start | bytes 786440 | tf_op jit(solution)/shard_map/ppermute | solution.py:286
  115.2 0.0 collective-permute-start.14
  115.2 16.9 %level0.1 = (bf16[512,256]{1,0:T(8,128)(2,1)S(1)}, bf16[512,256]{1,0:T(8,128)(2,1)S(1)}, f32[2,256,256]{2,1,0:T(8,128)S(1)}) custom-call(s32[2]{0:T(128)S(1)} %pad_add_fusion.place_ref, f32[256,384]{1,0:T(8,128)S(1)} %bitcast.20, f32[256,384]{1,0:T(8,128)S(1)} %collective-permute-done.8.refs_1_, f32[256,512]{1,0:T(8,128)S(1)} %constant_dynamic-update-slice_fusion.refs_2_, ...), custom_call_target="tpu_custom_call" | custom-call | flops 12000000000 | bytes 2097152 | tf_op jit(solution)/shard_map/level0/pallas_call | solution.py:124
  132.1 2.8 %collective-permute-start.10 = (bf16[1024,256]{1,0:T(8,128)(2,1)S(1)}, bf16[1024,256]{1,0:T(8,128)(2,1)S(1)}, u32[]{:S(2)}, u32[]{:S(2)}) collective-permute-start(bf16[1024,256]{1,0:T(8,128)(2,1)S(1)} %slice.63), channel_id=1, source_target_pairs={{0,192},{64,128},{128,64},{192,0},{1,193},{65,129},{129,65},{193,1... | collective-permute-start | bytes 1572872 | tf_op jit(solution)/shard_map/ppermute | solution.py:286
  134.9 0.0 collective-permute-start.11
  134.9 0.0 collective-permute-done.12.c1_ref
  134.9 0.0 collective-permute-done.14.c3_ref
  134.9 13.7 %level1.1.last_ref = bf16[64,512]{1,0:T(8,128)(2,1)S(1)} custom-call(s32[2]{0:T(128)S(1)} %pad_add_fusion.place_ref, bf16[512,256]{1,0:T(8,128)(2,1)S(1)} %get-tuple-element.45.near_ref, bf16[512,256]{1,0:T(8,128)(2,1)S(1)} %get-tuple-element.46.far_ref, f32[2,256,256]{2,1,0:T(8,128)S(1)} %get-tuple-element.47.outer_ref, ...), custom_call_target="tpu_custom_call" | custom-call | flops 8000000000 | bytes 2097152 | tf_op jit(solution)/shard_map/level1/pallas_call | solution.py:174
  148.7 0.0 collective-permute-done.11.p2b
  148.7 4.6 %rotate.1 = bf16[64,2048]{1,0:T(8,128)(2,1)} custom-call(bf16[2048,256]{1,0:T(8,128)(2,1)} %get-tuple-element.30.own, bf16[2048,256]{1,0:T(8,128)(2,1)S(1)} %collective-permute-done.3.p1, bf16[1024,256]{1,0:T(8,128)(2,1)S(1)} %collective-permute-done.10.p2a, bf16[1024,256]{1,0:T(8,128)(2,1)S(1)} %collective-permute-done.11.p2b, ...), custom_call_target="tpu_custom_call" | custom-call | tf_op jit(solution)/shard_map/rotate/pallas_call | solution.py:251
  (22 shorter events, 0.3 us)
Async XLA Ops:
  0.0 2.0 %copy-start = (s32[64,64]{1,0:T(8,128)S(1)}, s32[64,64]{1,0:T(8,128)}, u32[]{:S(2)}) copy-start(s32[64,64]{1,0:T(8,128)} %param.5) | copy-start | bytes 49156
  4.2 52.0 %all-to-all-start = ((bf16[64,48,256]{2,1,0:T(8,128)(2,1)}), bf16[64,48,256]{2,1,0:T(8,128)(2,1)S(1)}, u32[]{:S(2)}, u32[]{:S(2)}) async-start(bf16[64,48,256]{2,1,0:T(8,128)(2,1)} %bitcast.2), calls=%async_computation | async-start | bytes 3145728 | tf_op jit(solution)/shard_map/all_to_all | solution.py:301
  17.2 25.8 %collective-permute-start.1 = (bf16[2048,256]{1,0:T(8,128)(2,1)S(1)}, bf16[2048,256]{1,0:T(8,128)(2,1)}, u32[]{:S(2)}, u32[]{:S(2)}) collective-permute-start(bf16[2048,256]{1,0:T(8,128)(2,1)S(1)} %broadcast_select_fusion.rows_ref), channel_id=1, source_target_pairs={{0,192},{64,128},{128,64},{192,0},{1,193},{65,129},{129,65},{193,1... | collective-permute-start | bytes 3145736 | tf_op jit(solution)/shard_map/ppermute | solution.py:286
  20.0 24.1 %collective-permute-start = (bf16[2048,256]{1,0:T(8,128)(2,1)S(1)}, bf16[2048,256]{1,0:T(8,128)(2,1)}, u32[]{:S(2)}, u32[]{:S(2)}) collective-permute-start(bf16[2048,256]{1,0:T(8,128)(2,1)S(1)} %broadcast_select_fusion.rows_ref), channel_id=1, source_target_pairs={{0,64},{64,0},{128,192},{192,128},{1,65},{65,1},{129,193},{193,129... | collective-permute-start | bytes 3145736 | tf_op jit(solution)/shard_map/ppermute | solution.py:286
  47.7 3.1 %collective-permute-start.2 = (f32[256,384]{0,1:T(8,128)S(1)}, f32[256,384]{0,1:T(8,128)S(1)}, u32[]{:S(2)}, u32[]{:S(2)}) collective-permute-start(f32[256,384]{0,1:T(8,128)S(1)} %pad_maximum_fusion), channel_id=1, source_target_pairs={{0,1},{1,0},{2,3},{3,2},{4,5},{5,4},{6,7},{7,6},{8,9},{9,8},{10,11... | collective-permute-start | bytes 1179656 | tf_op jit(solution)/shard_map/ppermute | solution.py:289
  57.1 19.1 %all-to-all-start.1 = ((f32[32,8,384]{2,1,0:T(8,128)}), f32[32,8,384]{2,1,0:T(8,128)S(1)}, u32[]{:S(2)}, u32[]{:S(2)}) async-start(f32[32,8,384]{2,1,0:T(8,128)} %bitcast.3), calls=%async_computation.1 | async-start | bytes 786432 | tf_op jit(solution)/shard_map/all_to_all | solution.py:317
  64.9 23.8 %collective-permute-start.3 = (bf16[2048,256]{1,0:T(8,128)(2,1)}, bf16[2048,256]{1,0:T(8,128)(2,1)S(1)}, u32[]{:S(2)}, u32[]{:S(2)}) collective-permute-start(bf16[2048,256]{1,0:T(8,128)(2,1)} %get-tuple-element.30.own), channel_id=1, source_target_pairs={{0,64},{64,0},{128,192},{192,128},{1,65},{65,1},{129,193},{193,129... | collective-permute-start | bytes 3145736 | tf_op jit(solution)/shard_map/ppermute | solution.py:286
  66.2 24.7 %collective-permute-start.4 = (bf16[2048,256]{1,0:T(8,128)(2,1)}, bf16[2048,256]{1,0:T(8,128)(2,1)S(1)}, u32[]{:S(2)}, u32[]{:S(2)}) collective-permute-start(bf16[2048,256]{1,0:T(8,128)(2,1)} %get-tuple-element.32), channel_id=1, source_target_pairs={{0,192},{64,128},{128,64},{192,0},{1,193},{65,129},{129,65},{193,1... | collective-permute-start | bytes 3145736 | tf_op jit(solution)/shard_map/ppermute | solution.py:286
  77.0 17.8 %all-to-all-start.2 = ((f32[32,8,384]{2,1,0:T(8,128)}), f32[32,8,384]{2,1,0:T(8,128)S(1)}, u32[]{:S(2)}, u32[]{:S(2)}) async-start(f32[32,8,384]{2,1,0:T(8,128)} %broadcast_in_dim.18), calls=%async_computation.2 | async-start | bytes 786432 | tf_op jit(solution)/shard_map/all_to_all | solution.py:321
  94.8 7.5 %collective-permute-start.8 = (f32[256,384]{1,0:T(8,128)S(1)}, f32[256,384]{1,0:T(8,128)S(1)}, u32[]{:S(2)}, u32[]{:S(2)}) collective-permute-start(f32[256,384]{1,0:T(8,128)S(1)} %bitcast.17), channel_id=1, source_target_pairs={{0,1},{1,0},{2,3},{3,2},{4,5},{5,4},{6,7},{7,6},{8,9},{9,8},{10,11... | collective-permute-start | bytes 1179656 | tf_op jit(solution)/shard_map/ppermute | solution.py:289
  98.2 12.2 %collective-permute-start.7 = (f32[256,256]{1,0:T(8,128)S(1)}, f32[256,256]{1,0:T(8,128)S(1)}, u32[]{:S(2)}, u32[]{:S(2)}) collective-permute-start(f32[256,256]{1,0:T(8,128)S(1)} %slice.54), channel_id=1, source_target_pairs={{0,192},{64,128},{128,64},{192,0},{1,193},{65,129},{129,65},{193,1... | collective-permute-start | bytes 786440 | tf_op jit(solution)/shard_map/ppermute | solution.py:286
  101.0 4.9 %collective-permute-start.5 = (f32[256,128]{1,0:T(8,128)S(1)}, f32[256,128]{1,0:T(8,128)S(1)}, u32[]{:S(2)}, u32[]{:S(2)}) collective-permute-start(f32[256,128]{1,0:T(8,128)S(1)} %get-tuple-element.50), channel_id=1, source_target_pairs={{0,64},{64,0},{128,192},{192,128},{1,65},{65,1},{129,193},{193,129... | collective-permute-start | bytes 393224 | tf_op jit(solution)/shard_map/ppermute | solution.py:286
  101.1 7.5 %collective-permute-start.6 = (f32[256,128]{1,0:T(8,128)S(1)}, f32[256,128]{1,0:T(8,128)S(1)}, u32[]{:S(2)}, u32[]{:S(2)}) collective-permute-start(f32[256,128]{1,0:T(8,128)S(1)} %get-tuple-element.50), channel_id=1, source_target_pairs={{0,128},{64,192},{128,0},{192,64},{1,129},{65,193},{129,1},{193,65... | collective-permute-start | bytes 393224 | tf_op jit(solution)/shard_map/ppermute | solution.py:286
  110.4 4.8 %collective-permute-start.9 = (f32[256,512]{1,0:T(8,128)S(1)}, f32[256,512]{1,0:T(8,128)S(1)}, u32[]{:S(2)}, u32[]{:S(2)}) collective-permute-start(f32[256,512]{1,0:T(8,128)S(1)} %constant_dynamic-update-slice_fusion.refs_2_), channel_id=1, source_target_pairs={{0,1},{1,0},{2,3},{3,2},{4,5},{5,4},{6,7},{7,6},{8,9},{9,8},{10,11... | collective-permute-start | bytes 1572872 | tf_op jit(solution)/shard_map/ppermute | solution.py:289
  111.3 23.6 %copy-start.1 = (bf16[1024,256]{1,0:T(8,128)(2,1)S(1)}, bf16[1024,256]{1,0:T(8,128)(2,1)}, u32[]{:S(2)}) copy-start(bf16[1024,256]{1,0:T(8,128)(2,1)} %slice.64) | copy-start | bytes 1572868
  111.3 23.6 %collective-permute-start.12 = (f32[256,256]{1,0:T(8,128)S(1)}, f32[256,256]{1,0:T(8,128)S(1)}, u32[]{:S(2)}, u32[]{:S(2)}) collective-permute-start(f32[256,256]{1,0:T(8,128)S(1)} %maximum_select_fusion.c0_ref), channel_id=1, source_target_pairs={{0,64},{64,0},{128,192},{192,128},{1,65},{65,1},{129,193},{193,129... | collective-permute-start | bytes 786440 | tf_op jit(solution)/shard_map/ppermute | solution.py:286
  111.4 23.6 %collective-permute-start.13 = (f32[256,256]{1,0:T(8,128)S(1)}, f32[256,256]{1,0:T(8,128)S(1)}, u32[]{:S(2)}, u32[]{:S(2)}) collective-permute-start(f32[256,256]{1,0:T(8,128)S(1)} %maximum_select_fusion.c0_ref), channel_id=1, source_target_pairs={{0,128},{64,192},{128,0},{192,64},{1,129},{65,193},{129,1},{193,65... | collective-permute-start | bytes 786440 | tf_op jit(solution)/shard_map/ppermute | solution.py:286
  115.2 19.7 %collective-permute-start.14 = (f32[256,256]{1,0:T(8,128)S(1)}, f32[256,256]{1,0:T(8,128)S(1)}, u32[]{:S(2)}, u32[]{:S(2)}) collective-permute-start(f32[256,256]{1,0:T(8,128)S(1)} %maximum_select_fusion.c0_ref), channel_id=1, source_target_pairs={{0,192},{64,128},{128,64},{192,0},{1,193},{65,129},{129,65},{193,1... | collective-permute-start | bytes 786440 | tf_op jit(solution)/shard_map/ppermute | solution.py:286
  132.1 16.5 %collective-permute-start.10 = (bf16[1024,256]{1,0:T(8,128)(2,1)S(1)}, bf16[1024,256]{1,0:T(8,128)(2,1)S(1)}, u32[]{:S(2)}, u32[]{:S(2)}) collective-permute-start(bf16[1024,256]{1,0:T(8,128)(2,1)S(1)} %slice.63), channel_id=1, source_target_pairs={{0,192},{64,128},{128,64},{192,0},{1,193},{65,129},{129,65},{193,1... | collective-permute-start | bytes 1572872 | tf_op jit(solution)/shard_map/ppermute | solution.py:286
  134.9 13.8 %collective-permute-start.11 = (bf16[1024,256]{1,0:T(8,128)(2,1)S(1)}, bf16[1024,256]{1,0:T(8,128)(2,1)S(1)}, u32[]{:S(2)}, u32[]{:S(2)}) collective-permute-start(bf16[1024,256]{1,0:T(8,128)(2,1)S(1)} %copy-done.1), channel_id=1, source_target_pairs={{0,64},{64,0},{128,192},{192,128},{1,65},{65,1},{129,193},{193,129... | collective-permute-start | bytes 1572872 | tf_op jit(solution)/shard_map/ppermute | solution.py:286
